TPU v7x, 128 devices: a whole 4x4x4 slice. The times are simulated.
128 devices in a mesh: tm: 2 (over core), lon: 32 (over z, x, y_lo), cls: 2 (over y_hi).
Axes of the slice: x: 4, y: 4 (y_hi: 2, y_lo: 2; y = y_hi * 2 + y_lo), z: 4, core: 2. Of those that a mesh axis runs over, the one named last changes fastest.
Arguments:
- velocity: bfloat16 [32, 1024, 32, 256], P('tm', 'lon'), may hold values from -6 to 6
- thickness: bfloat16 [32, 1024, 32, 256], P('tm', 'lon'), may hold values from 0.25 to 4
- class_index: int32 [32, 1024, 32, 256], P('tm', 'lon'), may hold values from 0 to 238
- layer_weight: int32 [32, 1024, 32, 256], P('tm', 'lon'), may hold values from 0 to 64
- zonal_width: float32 [256], replicated, may hold values from 0.01 to 0.1
Outputs:
- psi_snap: float32 [32, 240, 256], P('tm', 'cls')
- psi_mean: float32 [240, 256], P('cls', ('tm', 'lon'))
- psi_var: float32 [240, 256], P('cls', ('tm', 'lon'))
All inputs are finite; a program needn't handle non-finite values.
Results may differ from a plain program's by a relative error of at most 0.0003.
Values sent between devices are 32-bit elements; how exact they have to be, the bound alone decides.
A program may use at most 128 MiB of HBM per device.

v0:
```python
import jax
import jax.numpy as jnp
from jax import lax
from jax.sharding import PartitionSpec as P

C = 240


def prefix(part, axis, combine, identity):
    place = lax.axis_index(axis)
    gathered = lax.all_gather(part, axis)
    state = jnp.zeros_like(part) + jnp.asarray(identity, part.dtype)

    def one(turn, state):
        return combine(state, lax.dynamic_index_in_dim(gathered, turn, 0, False))

    return lax.fori_loop(0, place, one, state)


def binning(velocity, thickness, class_index, layer_weight, zonal_width, class_low, class_dev):
    rows = velocity.shape[3]
    class_ids = lax.broadcasted_iota(jnp.int32, (class_dev, 1, rows), 0)

    def one_snapshot(items):
        speed, layer, lighter, share = items
        transport = speed.astype(jnp.float32) * layer.astype(jnp.float32) * zonal_width
        weight = share.astype(jnp.float32)
        first = (transport * (weight / 64.0)).reshape(1, -1, rows)
        second = (transport * ((64.0 - weight) / 64.0)).reshape(1, -1, rows)
        relative = (lighter - class_low).reshape(1, -1, rows)
        picked = jnp.where(relative == class_ids, first, 0.0) + jnp.where(
            relative + 1 == class_ids, second, 0.0
        )
        return jnp.sum(picked, axis=1)

    return lax.map(one_snapshot, (velocity, thickness, class_index, layer_weight))


def add_pair(earlier, later):
    return earlier + later


def shards(velocity, thickness, class_index, layer_weight, zonal_width):
    n_cls = lax.axis_size("cls")
    n_time = lax.axis_size("tm")
    n_lon = lax.axis_size("lon")
    class_dev = C // n_cls
    snaps = velocity.shape[0]
    rows = velocity.shape[3]
    block = rows // (n_time * n_lon)
    class_low = lax.axis_index("cls") * class_dev
    binned = binning(
        velocity, thickness, class_index, layer_weight, zonal_width, class_low, class_dev
    )
    zonal = lax.psum(binned, "lon")
    totals = jnp.sum(zonal, axis=1)
    offset = prefix(totals, "cls", add_pair, jnp.zeros_like(totals))
    psi = jnp.cumsum(zonal, axis=1) + offset[:, None, :]
    first_sum = jnp.sum(psi, axis=0)
    second_sum = jnp.sum(psi * psi, axis=0)
    sum_one, sum_two = (
        lax.psum_scatter(first_sum, "tm", scatter_dimension=1, tiled=True),
        lax.psum_scatter(second_sum, "tm", scatter_dimension=1, tiled=True),
    )
    start = lax.axis_index("lon") * block
    sum_one = lax.dynamic_slice_in_dim(sum_one, start, block, 1)
    sum_two = lax.dynamic_slice_in_dim(sum_two, start, block, 1)
    count = snaps * n_time
    psi_mean = sum_one / count
    psi_var = sum_two / count - psi_mean * psi_mean
    return (psi, psi_mean, psi_var)


def solution(mesh):
    in_specs = (
        P("tm", "lon", None, None),
        P("tm", "lon", None, None),
        P("tm", "lon", None, None),
        P("tm", "lon", None, None),
        P(),
    )
    out_specs = (P("tm", "cls", None), P("cls", ("tm", "lon")), P("cls", ("tm", "lon")))
    return jax.shard_map(shards, mesh=mesh, in_specs=in_specs, out_specs=out_specs, check_vma=False)
```

profile of v0, /device:TPU:1, one launch (start us, length us, event | category | flops | bytes accessed | tf_op | source)
XLA Modules:
  0.0 837.1 jit_solution(16211556044976445368)
XLA Ops:
  7.2 472.6 %while.23 = (s32[]{:T(128)}, f32[16,120,256]{2,1,0:T(8,128)S(1)}, s32[16,32,32,256]{3,2,1,0:T(8,128)}, s32[]{:T(128)}, bf16[16,32,32,256]{3,2,1,0:T(8,128)(2,1)}...) while((s32[]{:T(128)}, f32[16,120,256]{2,1,0:T(8,128)S(1)}, ...), condition=%wide.region_2.3_spmd.clone.clone, body=%wide.region_0.2_spmd.clone.clone.sunk | while | flops 191858688 | bytes 19244140 | solution.py:36
  7.2 2.0 convert_multiply_fusion.3
  11.5 25.3 %add_reduce_fusion.2 = f32[120,256]{1,0:T(8,128)S(1)} fusion(f32[1024,256]{1,0:T(8,128)S(1)} %get-tuple-element.244, s32[1024,256]{1,0:T(8,128)S(1)} %broadcast_add_fusion.3, f32[1024,256]{1,0:T(8,128)S(1)} %get-tuple-element.245, s32[1024,256]{1,0:T(8,128)S(1)} %bitcast.29), kind=kLoop, calls=%fused_computation.4.clone.1 | loop fusion | flops 188712960 | bytes 4317184 | tf_op jit(solution)/shard_map/while/body/eval_jaxpr/reduce_sum | solution.py:34
  36.8 2.0 convert_multiply_fusion.3
  39.6 1.3 dynamic-slice_subtract_fusion.2
  41.0 25.3 %add_reduce_fusion.2 = f32[120,256]{1,0:T(8,128)S(1)} fusion(f32[1024,256]{1,0:T(8,128)S(1)} %get-tuple-element.244, s32[1024,256]{1,0:T(8,128)S(1)} %broadcast_add_fusion.3, f32[1024,256]{1,0:T(8,128)S(1)} %get-tuple-element.245, s32[1024,256]{1,0:T(8,128)S(1)} %bitcast.29), kind=kLoop, calls=%fused_computation.4.clone.1 | loop fusion | flops 188712960 | bytes 4317184 | tf_op jit(solution)/shard_map/while/body/eval_jaxpr/reduce_sum | solution.py:34
  66.3 2.0 convert_multiply_fusion.3
  69.1 1.3 dynamic-slice_subtract_fusion.2
  70.5 25.3 %add_reduce_fusion.2 = f32[120,256]{1,0:T(8,128)S(1)} fusion(f32[1024,256]{1,0:T(8,128)S(1)} %get-tuple-element.244, s32[1024,256]{1,0:T(8,128)S(1)} %broadcast_add_fusion.3, f32[1024,256]{1,0:T(8,128)S(1)} %get-tuple-element.245, s32[1024,256]{1,0:T(8,128)S(1)} %bitcast.29), kind=kLoop, calls=%fused_computation.4.clone.1 | loop fusion | flops 188712960 | bytes 4317184 | tf_op jit(solution)/shard_map/while/body/eval_jaxpr/reduce_sum | solution.py:34
  95.9 2.0 convert_multiply_fusion.3
  98.7 1.3 dynamic-slice_subtract_fusion.2
  100.1 25.3 %add_reduce_fusion.2 = f32[120,256]{1,0:T(8,128)S(1)} fusion(f32[1024,256]{1,0:T(8,128)S(1)} %get-tuple-element.244, s32[1024,256]{1,0:T(8,128)S(1)} %broadcast_add_fusion.3, f32[1024,256]{1,0:T(8,128)S(1)} %get-tuple-element.245, s32[1024,256]{1,0:T(8,128)S(1)} %bitcast.29), kind=kLoop, calls=%fused_computation.4.clone.1 | loop fusion | flops 188712960 | bytes 4317184 | tf_op jit(solution)/shard_map/while/body/eval_jaxpr/reduce_sum | solution.py:34
  125.4 2.0 convert_multiply_fusion.3
  128.2 1.3 dynamic-slice_subtract_fusion.2
  129.6 25.3 %add_reduce_fusion.2 = f32[120,256]{1,0:T(8,128)S(1)} fusion(f32[1024,256]{1,0:T(8,128)S(1)} %get-tuple-element.244, s32[1024,256]{1,0:T(8,128)S(1)} %broadcast_add_fusion.3, f32[1024,256]{1,0:T(8,128)S(1)} %get-tuple-element.245, s32[1024,256]{1,0:T(8,128)S(1)} %bitcast.29), kind=kLoop, calls=%fused_computation.4.clone.1 | loop fusion | flops 188712960 | bytes 4317184 | tf_op jit(solution)/shard_map/while/body/eval_jaxpr/reduce_sum | solution.py:34
  154.9 2.0 convert_multiply_fusion.3
  157.8 1.3 dynamic-slice_subtract_fusion.2
  159.1 25.3 %add_reduce_fusion.2 = f32[120,256]{1,0:T(8,128)S(1)} fusion(f32[1024,256]{1,0:T(8,128)S(1)} %get-tuple-element.244, s32[1024,256]{1,0:T(8,128)S(1)} %broadcast_add_fusion.3, f32[1024,256]{1,0:T(8,128)S(1)} %get-tuple-element.245, s32[1024,256]{1,0:T(8,128)S(1)} %bitcast.29), kind=kLoop, calls=%fused_computation.4.clone.1 | loop fusion | flops 188712960 | bytes 4317184 | tf_op jit(solution)/shard_map/while/body/eval_jaxpr/reduce_sum | solution.py:34
  184.5 2.0 convert_multiply_fusion.3
  187.3 1.3 dynamic-slice_subtract_fusion.2
  188.7 25.3 %add_reduce_fusion.2 = f32[120,256]{1,0:T(8,128)S(1)} fusion(f32[1024,256]{1,0:T(8,128)S(1)} %get-tuple-element.244, s32[1024,256]{1,0:T(8,128)S(1)} %broadcast_add_fusion.3, f32[1024,256]{1,0:T(8,128)S(1)} %get-tuple-element.245, s32[1024,256]{1,0:T(8,128)S(1)} %bitcast.29), kind=kLoop, calls=%fused_computation.4.clone.1 | loop fusion | flops 188712960 | bytes 4317184 | tf_op jit(solution)/shard_map/while/body/eval_jaxpr/reduce_sum | solution.py:34
  214.0 2.0 convert_multiply_fusion.3
  216.8 1.3 dynamic-slice_subtract_fusion.2
  218.2 25.3 %add_reduce_fusion.2 = f32[120,256]{1,0:T(8,128)S(1)} fusion(f32[1024,256]{1,0:T(8,128)S(1)} %get-tuple-element.244, s32[1024,256]{1,0:T(8,128)S(1)} %broadcast_add_fusion.3, f32[1024,256]{1,0:T(8,128)S(1)} %get-tuple-element.245, s32[1024,256]{1,0:T(8,128)S(1)} %bitcast.29), kind=kLoop, calls=%fused_computation.4.clone.1 | loop fusion | flops 188712960 | bytes 4317184 | tf_op jit(solution)/shard_map/while/body/eval_jaxpr/reduce_sum | solution.py:34
  243.6 2.0 convert_multiply_fusion.3
  246.4 1.3 dynamic-slice_subtract_fusion.2
  247.8 25.3 %add_reduce_fusion.2 = f32[120,256]{1,0:T(8,128)S(1)} fusion(f32[1024,256]{1,0:T(8,128)S(1)} %get-tuple-element.244, s32[1024,256]{1,0:T(8,128)S(1)} %broadcast_add_fusion.3, f32[1024,256]{1,0:T(8,128)S(1)} %get-tuple-element.245, s32[1024,256]{1,0:T(8,128)S(1)} %bitcast.29), kind=kLoop, calls=%fused_computation.4.clone.1 | loop fusion | flops 188712960 | bytes 4317184 | tf_op jit(solution)/shard_map/while/body/eval_jaxpr/reduce_sum | solution.py:34
  273.1 2.0 convert_multiply_fusion.3
  277.3 25.3 %add_reduce_fusion.2 = f32[120,256]{1,0:T(8,128)S(1)} fusion(f32[1024,256]{1,0:T(8,128)S(1)} %get-tuple-element.244, s32[1024,256]{1,0:T(8,128)S(1)} %broadcast_add_fusion.3, f32[1024,256]{1,0:T(8,128)S(1)} %get-tuple-element.245, s32[1024,256]{1,0:T(8,128)S(1)} %bitcast.29), kind=kLoop, calls=%fused_computation.4.clone.1 | loop fusion | flops 188712960 | bytes 4317184 | tf_op jit(solution)/shard_map/while/body/eval_jaxpr/reduce_sum | solution.py:34
  302.6 2.0 convert_multiply_fusion.3
  306.8 25.3 %add_reduce_fusion.2 = f32[120,256]{1,0:T(8,128)S(1)} fusion(f32[1024,256]{1,0:T(8,128)S(1)} %get-tuple-element.244, s32[1024,256]{1,0:T(8,128)S(1)} %broadcast_add_fusion.3, f32[1024,256]{1,0:T(8,128)S(1)} %get-tuple-element.245, s32[1024,256]{1,0:T(8,128)S(1)} %bitcast.29), kind=kLoop, calls=%fused_computation.4.clone.1 | loop fusion | flops 188712960 | bytes 4317184 | tf_op jit(solution)/shard_map/while/body/eval_jaxpr/reduce_sum | solution.py:34
  332.2 2.0 convert_multiply_fusion.3
  336.4 25.3 %add_reduce_fusion.2 = f32[120,256]{1,0:T(8,128)S(1)} fusion(f32[1024,256]{1,0:T(8,128)S(1)} %get-tuple-element.244, s32[1024,256]{1,0:T(8,128)S(1)} %broadcast_add_fusion.3, f32[1024,256]{1,0:T(8,128)S(1)} %get-tuple-element.245, s32[1024,256]{1,0:T(8,128)S(1)} %bitcast.29), kind=kLoop, calls=%fused_computation.4.clone.1 | loop fusion | flops 188712960 | bytes 4317184 | tf_op jit(solution)/shard_map/while/body/eval_jaxpr/reduce_sum | solution.py:34
  361.7 2.0 convert_multiply_fusion.3
  365.9 25.3 %add_reduce_fusion.2 = f32[120,256]{1,0:T(8,128)S(1)} fusion(f32[1024,256]{1,0:T(8,128)S(1)} %get-tuple-element.244, s32[1024,256]{1,0:T(8,128)S(1)} %broadcast_add_fusion.3, f32[1024,256]{1,0:T(8,128)S(1)} %get-tuple-element.245, s32[1024,256]{1,0:T(8,128)S(1)} %bitcast.29), kind=kLoop, calls=%fused_computation.4.clone.1 | loop fusion | flops 188712960 | bytes 4317184 | tf_op jit(solution)/shard_map/while/body/eval_jaxpr/reduce_sum | solution.py:34
  391.3 2.0 convert_multiply_fusion.3
  395.5 25.3 %add_reduce_fusion.2 = f32[120,256]{1,0:T(8,128)S(1)} fusion(f32[1024,256]{1,0:T(8,128)S(1)} %get-tuple-element.244, s32[1024,256]{1,0:T(8,128)S(1)} %broadcast_add_fusion.3, f32[1024,256]{1,0:T(8,128)S(1)} %get-tuple-element.245, s32[1024,256]{1,0:T(8,128)S(1)} %bitcast.29), kind=kLoop, calls=%fused_computation.4.clone.1 | loop fusion | flops 188712960 | bytes 4317184 | tf_op jit(solution)/shard_map/while/body/eval_jaxpr/reduce_sum | solution.py:34
  420.8 2.0 convert_multiply_fusion.3
  425.0 25.3 %add_reduce_fusion.2 = f32[120,256]{1,0:T(8,128)S(1)} fusion(f32[1024,256]{1,0:T(8,128)S(1)} %get-tuple-element.244, s32[1024,256]{1,0:T(8,128)S(1)} %broadcast_add_fusion.3, f32[1024,256]{1,0:T(8,128)S(1)} %get-tuple-element.245, s32[1024,256]{1,0:T(8,128)S(1)} %bitcast.29), kind=kLoop, calls=%fused_computation.4.clone.1 | loop fusion | flops 188712960 | bytes 4317184 | tf_op jit(solution)/shard_map/while/body/eval_jaxpr/reduce_sum | solution.py:34
  450.3 2.0 convert_multiply_fusion.3
  454.5 25.3 %add_reduce_fusion.2 = f32[120,256]{1,0:T(8,128)S(1)} fusion(f32[1024,256]{1,0:T(8,128)S(1)} %get-tuple-element.244, s32[1024,256]{1,0:T(8,128)S(1)} %broadcast_add_fusion.3, f32[1024,256]{1,0:T(8,128)S(1)} %get-tuple-element.245, s32[1024,256]{1,0:T(8,128)S(1)} %bitcast.29), kind=kLoop, calls=%fused_computation.4.clone.1 | loop fusion | flops 188712960 | bytes 4317184 | tf_op jit(solution)/shard_map/while/body/eval_jaxpr/reduce_sum | solution.py:34
  481.2 291.7 %all-reduce.2.cloned.1.call-done = f32[16,120,256]{2,1,0:T(8,128)} async-done(((f32[16,120,256]{2,1,0:T(8,128)}), f32[16,120,256]{2,1,0:T(8,128)}) %all-reduce.2.cloned.1.call-update) | async-done | bytes 1966096 | tf_op jit(solution)/shard_map/psum | solution.py:55
  772.9 1.7 reduce_sum.36
  774.6 5.4 all-gather
  780.0 3.4 multiply_reduce_fusion
  785.0 2.4 copy.17
  787.4 27.9 %reduce-scatter.3.cloned.1.call-done = f32[120,128]{0,1:T(8,128)} async-done(((f32[120,256]{0,1:T(8,128)}), f32[120,128]{0,1:T(8,128)}) %reduce-scatter.3.cloned.1.call-update) | async-done | bytes 61456 | tf_op jit(solution)/shard_map/reduce_scatter | solution.py:62
  815.3 14.0 %reduce-scatter.5.cloned.1.call-done = f32[120,128]{0,1:T(8,128)} async-done(((f32[120,256]{0,1:T(8,128)}), f32[120,128]{0,1:T(8,128)}) %reduce-scatter.5.cloned.1.call-update) | async-done | bytes 61456 | tf_op jit(solution)/shard_map/reduce_scatter | solution.py:63
  (70 shorter events, 29.7 us)
Async XLA Ops:
  7.2 765.7 %all-reduce.2.cloned.1.call-start = ((), (), s32[]{:S(2)}) async-start(), calls=%async_computation.2 | async-start | bytes 3932160 | tf_op jit(solution)/shard_map/psum | solution.py:55
  479.9 1.3 copy-start
  481.2 334.1 %reduce-scatter.3.cloned.1.call-start = ((), (), s32[]{:S(2)}) async-start(), calls=%async_computation.3 | async-start | bytes 196608 | tf_op jit(solution)/shard_map/reduce_scatter | solution.py:62
  784.2 45.1 %reduce-scatter.5.cloned.1.call-start = ((), (), s32[]{:S(2)}) async-start(), calls=%async_computation.4 | async-start | bytes 196608 | tf_op jit(solution)/shard_map/reduce_scatter | solution.py:63
Sparse Core Ops, SparseCore 0:
  481.3 291.5 all-reduce.1
  784.3 30.9 reduce-scatter.2
  817.7 11.5 reduce-scatter.4
where the time goes:
time: 839 us; the launch traced here: 837 us
  other arithmetic  478 us (57%)
  waiting for transfers between devices  334 us (40%)
  between operations  13.8 us (2%)
    reduce_sum x16, other arithmetic, one_snapshot(): return jnp.sum(picked, axis=1)  404 us
    psum x1, waiting for transfers between devices, shards(): zonal = lax.psum(binned, 'lon')  292 us
    div x16, other arithmetic, one_snapshot(): first = (transport * (weight / 64.0)).reshape(1, -1, rows)  31.3 us
    reduce_scatter x1, waiting for transfers between devices, shards(): lax.psum_scatter(first_sum, 'tm', scatter_dimension=1, tiled=True)  27.9 us
    sub x16, other arithmetic, one_snapshot(): relative = (lighter - class_low).reshape(1, -1, rows)  20.9 us
  transfers between devices with their start and end apart: 3, of which 3 were waited for; matrix products, arithmetic and copies ran while one was open for 0% of the time, Pallas kernels for 0%

commit v1 on v0

v1 whole, which is shorter than its diff:
```python
import functools
import jax
import jax.numpy as jnp
from jax import lax
from jax.experimental import pallas as pl
from jax.experimental.pallas import tpu as pltpu
from jax.sharding import PartitionSpec as P

C = 240
GROUPS = 8
NT = (((1,), (1,)), ((), ()))
MESH = pl.DeviceIdType.MESH
F32, BF16 = jnp.float32, jnp.bfloat16


def prepare(raw, turned, chunk):
    lons = pl.ds(chunk * 8, 8)
    cells = pl.ds(pl.multiple_of(chunk * 256, 256), 256)
    speed, layer, lighter, share = (ref[lons].reshape(256, 256) for ref in raw)
    v_t, h_t, hi_t, lo_t, q_t, e_t = turned
    v_t[:, cells] = speed.T
    h_t[:, cells] = layer.T
    k = lighter.astype(F32)
    hi = jnp.floor(k * (1 / 15.0) + (1 / 30.0))
    hi_t[:, cells] = hi.astype(BF16).T
    lo_t[:, cells] = (k - hi * 15.0).astype(BF16).T
    part = layer.astype(F32) * (share.astype(F32) * (1 / 64.0))
    q = part.astype(BF16)
    q_t[:, cells] = q.T
    e_t[:, cells] = (part - q.astype(F32)).astype(BF16).T


def group_sums(turned, rows, diagonal):
    total = None
    for start in range(0, 1024, 256):
        cells = slice(start, start + 256)
        v, h, hi, lo, q, e = (ref[rows, cells] for ref in turned)
        zero = jnp.zeros_like(v)
        a = jnp.concatenate([jnp.where(hi == float(x), v, zero) for x in range(16)], axis=0)
        b, f = [], []
        below = zero
        for x in range(15):
            here = lo == float(x)
            b.append(jnp.where(here, q, below))
            f.append(jnp.where(here, e, zero))
            below = jnp.where(here, h, below)
        b = jnp.concatenate(b + [below], axis=0)
        f = jnp.concatenate(f + [zero], axis=0)
        part = lax.dot_general(
            jnp.concatenate([a, a], axis=1),
            jnp.concatenate([b, f], axis=1),
            NT,
            preferred_element_type=F32,
        )
        total = part if total is None else total + part
    return jnp.where(diagonal[None], total.reshape(16, 16, 256), 0.0).sum(1)


def arrange(sums, width, units, unit_of):
    lane = lax.broadcasted_iota(jnp.int32, (16, 128), 1)
    slot = [[None, None] for _ in range(16)]
    for half in range(2):
        for part in range(2):
            x = [sums[half * 8 + g, :, part * 128 : part * 128 + 128] for g in range(8)]
            for d in (4, 2, 1):
                high = (lane & (16 * d)) != 0
                y = list(x)
                for i in range(8):
                    if i & d == 0:
                        y[i] = jnp.where(high, pltpu.roll(x[i + d], 16 * d, 1), x[i])
                        y[i + d] = jnp.where(high, x[i + d], pltpu.roll(x[i], 128 - 16 * d, 1))
                x = y
            for i in range(8):
                slot[part * 8 + i][half] = x[i]
    hi = lax.broadcasted_iota(jnp.int32, (16, 128), 0)
    for half in range(2):
        whole = slot[15][half]
        run = whole
        for d in (1, 2, 4, 8):
            run = run + jnp.where(hi >= d, pltpu.roll(run, d, 0), 0.0)
        offset = run - whole
        z = width[:, half * 128 : half * 128 + 128]
        for x in range(15):
            y = (slot[x][half] + offset) * z
            for cut in range(2):
                units[unit_of(cut, half), pl.ds(x, 8, stride=15), :] = y[cut * 8 : cut * 8 + 8]


def kernel(comm, v_hbm, h_hbm, k_hbm, w_hbm, width, psi_hbm, mean_ref, var_ref, *scratch):
    (raw_v, raw_h, raw_k, raw_w), scratch = scratch[:4], scratch[4:]
    even, odd, scratch = scratch[:6], scratch[6:12], scratch[12:]
    (sums, send, got_1, mid, got_2, own, pad, stat, got_3, read_sem, write_sem) = scratch[:11]
    (s1, r1, s2, r2, s3, r3, s4, r4, s5, r5) = scratch[11:]
    if comm:
        tm, lon, cls = lax.axis_index("tm"), lax.axis_index("lon"), lax.axis_index("cls")
    else:
        tm, lon, cls = jnp.int32(0), jnp.int32(0), jnp.int32(0)
    zz, xx, yy = lon // 8, (lon // 2) % 4, lon % 2
    n_own = 8

    def read(s, slot):
        return [
            pltpu.make_async_copy(src.at[cls * n_own + s], dst.at[slot], read_sem.at[slot, i])
            for i, (src, dst) in enumerate(
                zip((v_hbm, h_hbm, k_hbm, w_hbm), (raw_v, raw_h, raw_k, raw_w))
            )
        ]

    def lon_of(p, a, b, y):
        return a * 8 + b * 2 + y if p else b * 8 + a * 2 + y

    def spot(p):
        return (zz, xx) if p else (xx, zz)

    def first(p, s, rel):
        a, b = spot(p)
        to = (a + rel) % 4
        return pltpu.make_async_remote_copy(
            src_ref=send.at[s, to], dst_ref=got_1.at[s, 3 - rel], send_sem=s1.at[s, rel - 1],
            recv_sem=r1.at[s, 3 - rel], device_id={"lon": lon_of(p, to, b, yy)}, device_id_type=MESH)

    def second(p, s, rel):
        a, b = spot(p)
        to = (b * 2 + yy + rel) % 8
        return pltpu.make_async_remote_copy(
            src_ref=mid.at[s, pl.ds(pl.multiple_of(to * 16, 16), 16)], dst_ref=got_2.at[s, 7 - rel],
            send_sem=s2.at[s, rel - 1], recv_sem=r2.at[s, 7 - rel],
            device_id={"lon": lon_of(p, a, to // 2, to % 2)}, device_id_type=MESH)

    def unit_at(p, a):
        home = (cls + a // 2) % 2
        return home * n_own, a % 2

    def third(p, s, rel):
        a, b = spot(p)
        me = b * 2 + yy
        to = (me + rel) % 8
        rows = pl.ds(pl.multiple_of(me * 16, 16), 16)
        return pltpu.make_async_remote_copy(
            src_ref=own.at[s], dst_ref=pad.at[cls * n_own + s, a % 2, rows],
            send_sem=s3.at[s, rel], recv_sem=r3.at[s, (8 - rel) % 8],
            device_id={"lon": lon_of(p, a, to // 2, to % 2), "cls": (cls + a // 2) % 2},
            device_id_type=MESH)

    def third_got(p, s, rel):
        a, b = spot(p)
        base, half = unit_at(p, a)
        frm = (b * 2 + yy + rel) % 8
        rows = pl.ds(pl.multiple_of(frm * 16, 16), 16)
        dst = pad.at[base + s, half, rows]
        return pltpu.make_async_remote_copy(
            src_ref=own.at[s], dst_ref=dst, send_sem=s3.at[s, rel], recv_sem=r3.at[s, rel],
            device_id={"lon": lon_of(p, a, frm // 2, frm % 2), "cls": (cls + a // 2) % 2},
            device_id_type=MESH)

    def fourth(p, s, rel):
        a, b = spot(p)
        base, half = unit_at(p, a)
        return pltpu.make_async_remote_copy(
            src_ref=pad.at[base + s, half], dst_ref=pad.at[base + s, half], send_sem=s4.at[s, rel - 1],
            recv_sem=r4.at[s, 3 - rel], device_id={"lon": lon_of(p, (a + rel) % 4, b, yy)},
            device_id_type=MESH)

    def fourth_got(p, s, rel):
        a, b = spot(p)
        frm = (a + rel) % 4
        base, half = unit_at(p, frm)
        dst = pad.at[base + s, half]
        return pltpu.make_async_remote_copy(
            src_ref=dst, dst_ref=dst, send_sem=s4.at[s, rel - 1], recv_sem=r4.at[s, rel - 1],
            device_id={"lon": lon_of(p, frm, b, yy)}, device_id_type=MESH)

    def write(s):
        return [
            pltpu.make_async_copy(
                pad.at[base + s, half, pl.ds(0, C // 2)],
                psi_hbm.at[base + s, :, pl.ds(half * 128, 128)],
                write_sem.at[s, base // 4 + half])
            for base in (0, n_own) for half in (0, 1)
        ]

    def start_1(p, s):
        for rel in (1, 2, 3):
            first(p, s, rel).start()

    def start_2(p, s):
        a, _ = spot(p)
        for rel in (1, 2, 3):
            first(p, s, 4 - rel).wait_recv()
        mid[s] = send[s, a] + got_1[s, 0] + got_1[s, 1] + got_1[s, 2]
        for rel in range(1, 8):
            second(p, s, rel).start()

    def start_3(p, s):
        a, b = spot(p)
        me = b * 2 + yy
        rows = pl.ds(pl.multiple_of(me * 16, 16), 16)
        for rel in range(1, 8):
            second(p, s, 8 - rel).wait_recv()
        total = mid[s, rows]
        for i in range(7):
            total = total + got_2[s, i]
        own[s] = total

        @pl.when(a < 2)
        def _():
            pad[cls * n_own + s, a % 2, rows] = total

        @pl.when(a >= 2)
        def _():
            third(p, s, 0).start()

        for rel in range(1, 8):
            third(p, s, rel).start()

    def start_4(p, s):
        a, _ = spot(p)

        @pl.when(a >= 2)
        def _():
            third_got(p, s, 0).wait_recv()

        for rel in range(1, 8):
            third_got(p, s, rel).wait_recv()
        for rel in (1, 2, 3):
            fourth(p, s, rel).start()

    def take(s):
        for half in range(2):
            one, two = stat[half, 0], stat[half, 1]
            for base in (0, n_own):
                x = pad[base + s, half]
                one = one + x
                two = two + x * x
            stat[half, 0] = one
            stat[half, 1] = two

    def finish(p, s):
        for rel in (1, 2, 3):
            fourth_got(p, s, rel).wait_recv()
        for copy in write(s):
            copy.start()
        take(s)

    def drain(p, s):
        a, _ = spot(p)
        for rel in (1, 2, 3):
            first(p, s, rel).wait_send()
            fourth(p, s, rel).wait_send()
        for rel in range(1, 8):
            second(p, s, rel).wait_send()
            third(p, s, rel).wait_send()

        @pl.when(a >= 2)
        def _():
            third(p, s, 0).wait_send()

        for copy in write(s):
            copy.wait()

    barrier = None
    if comm:
        barrier = pltpu.get_barrier_semaphore()
        def greet(to, where):
            pl.semaphore_signal(barrier, inc=1, device_id=where, device_id_type=MESH)

        for y in range(2):
            for i in range(4):
                for near in range(2):
                    group = (cls + near) % 2
                    row = {"lon": ((zz + i) % 4) * 8 + xx * 2 + (yy + y) % 2, "cls": group}
                    if near or i or y:
                        greet(None, row)
                    if i:
                        greet(None, {"lon": zz * 8 + ((xx + i) % 4) * 2 + (yy + y) % 2, "cls": group})
        greet(None, {"tm": 1 - tm})
    n_greet = 2 * 2 * 4 - 1 + 2 * 2 * 3 + 1

    lane = lax.broadcasted_iota(jnp.int32, (16, 256), 1)
    row = lax.broadcasted_iota(jnp.int32, (16, 256), 0)
    diagonal = (lane & 15) == row
    raws = [[ref.at[slot] for ref in (raw_v, raw_h, raw_k, raw_w)] for slot in range(2)]

    for copy in read(0, 0):
        copy.start()
    for copy in read(1, 1):
        copy.start()
    stat[...] = jnp.zeros_like(stat)
    for copy in read(0, 0):
        copy.wait()

    def prologue(chunk, carry):
        prepare(raws[0], even, chunk)
        return carry

    lax.fori_loop(0, 4, prologue, 0)

    def compute(s, p):
        here, there = (odd, even) if p else (even, odd)

        @pl.when(s + 2 < n_own)
        def _():
            for copy in read(s + 2, p):
                copy.start()

        @pl.when(s + 1 < n_own)
        def _():
            for copy in read(s + 1, 1 - p):
                copy.wait()

        def step(j, carry):
            for c in range(GROUPS // 4):
                prepare(raws[1 - p], there, j * (GROUPS // 4) + c)
            for g in range(GROUPS):
                at = j * GROUPS + g
                rows = pl.ds(pl.multiple_of(at * 16, 16), 16)
                sums[at] = group_sums(here, rows, diagonal)
            return carry

        lax.fori_loop(0, 16 // GROUPS, step, 0)
        units = send.at[s]
        for u in range(4):
            units[u, pl.ds(C // 2, 8), :] = jnp.zeros((8, 128), F32)
        arrange(sums, width[...], units, lambda cut, half: ((cls + cut) % 2) * 2 + half)

    def pair(t, carry):
        for p in range(2):
            s = 2 * t + p
            compute(s, p)
            if not comm:
                continue
            if p == 0:
                @pl.when(t == 0)
                def _():
                    pl.semaphore_wait(barrier, n_greet)
            start_1(p, s)

            def guard(least, go, q, back):
                if least <= p:
                    go(q, s - back)
                else:
                    @pl.when(s >= least)
                    def _():
                        go(q, s - back)

            guard(1, start_2, 1 - p, 1)
            guard(2, start_3, p, 2)
            guard(3, start_4, 1 - p, 3)
            guard(4, finish, p, 4)
        return carry

    lax.fori_loop(0, n_own // 2, pair, 0)
    if comm:
        start_2(1, 7)
        start_3(0, 6)
        start_4(1, 5)
        finish(0, 4)
        start_3(1, 7)
        start_4(0, 6)
        finish(1, 5)
        start_4(1, 7)
        finish(0, 6)
        finish(1, 7)
        swap = pltpu.make_async_remote_copy(
            src_ref=stat.at[1 - tm], dst_ref=got_3, send_sem=s5, recv_sem=r5,
            device_id={"tm": 1 - tm}, device_id_type=MESH)
        swap.start()
        def drains(t, carry):
            drain(0, 2 * t)
            drain(1, 2 * t + 1)
            return carry
        lax.fori_loop(0, n_own // 2, drains, 0)
        swap.wait()
    else:
        for s in range(8):
            pad[s, 0] = send[s, 0]
            pad[s, 1] = send[s, 1]
            pad[s + 8, 0] = send[s, 2]
            pad[s + 8, 1] = send[s, 3]
            for copy in write(s):
                copy.start()
            for copy in write(s):
                copy.wait()
        got_3[...] = jnp.zeros_like(got_3)
    count = 32.0
    mean = (stat[tm, 0] + got_3[0]) / count
    var = (stat[tm, 1] + got_3[1]) / count - mean * mean
    mean_ref[...] = pltpu.roll(mean, (128 - lon * 4) % 128, 1)[: C // 2, :4]
    var_ref[...] = pltpu.roll(var, (128 - lon * 4) % 128, 1)[: C // 2, :4]


def overturning(v, h, k, w, width, comm=True):
    dma = pltpu.SemaphoreType.DMA
    hbm = pl.BlockSpec(memory_space=pl.ANY)
    vmem = pl.BlockSpec(memory_space=pltpu.VMEM)
    scratch = [pltpu.VMEM((2, 32, 32, 256), d) for d in (BF16, BF16, jnp.int32, jnp.int32)]
    scratch += [pltpu.VMEM((256, 1024), BF16)] * 12
    scratch += [
        pltpu.VMEM((16, 16, 256), F32),
        pltpu.VMEM((8, 4, 128, 128), F32),
        pltpu.VMEM((8, 3, 128, 128), F32),
        pltpu.VMEM((8, 128, 128), F32),
        pltpu.VMEM((8, 7, 16, 128), F32),
        pltpu.VMEM((8, 16, 128), F32),
        pltpu.VMEM((16, 2, 128, 128), F32),
        pltpu.VMEM((2, 2, 128, 128), F32),
        pltpu.VMEM((2, 128, 128), F32),
        dma((2, 4)), dma((8, 4)),
        dma((8, 3)), dma((8, 3)), dma((8, 7)), dma((8, 7)),
        dma((8, 8)), dma((8, 8)), dma((8, 3)), dma((8, 3)), dma, dma,
    ]
    return pl.pallas_call(
        functools.partial(kernel, comm),
        in_specs=[hbm] * 4 + [vmem],
        out_specs=(hbm, vmem, vmem),
        out_shape=(
            jax.ShapeDtypeStruct((16, C // 2, 256), F32),
            jax.ShapeDtypeStruct((C // 2, 4), F32),
            jax.ShapeDtypeStruct((C // 2, 4), F32),
        ),
        scratch_shapes=scratch,
        compiler_params=pltpu.CompilerParams(
            vmem_limit_bytes=56 * 2**20,
            **(dict(collective_id=0, has_side_effects=True) if comm else {}),
        ),
        name="overturning",
    )(v, h, k, w, width)


def shards(velocity, thickness, class_index, layer_weight, zonal_width):
    return overturning(velocity, thickness, class_index, layer_weight, zonal_width.reshape(1, -1))


def solution(mesh):
    cells = P("tm", "lon", None, None)
    in_specs = (cells, cells, cells, cells, P())
    out_specs = (P("tm", "cls", None), P("cls", ("tm", "lon")), P("cls", ("tm", "lon")))
    return jax.shard_map(shards, mesh=mesh, in_specs=in_specs, out_specs=out_specs, check_vma=False)
```

time: 839 us -> 89.4 us (0.11)
  other arithmetic: 478 us -> 0 us
  waiting for transfers between devices: 334 us -> 0 us
  Pallas kernels: 0 us -> 82.6 us
  between operations: 13.8 us -> 0.64 us
    reduce_sum x17 -> x0, other arithmetic: 406 us -> none  [the longest x16 404 us: one_snapshot(): return jnp.sum(picked, axis=1)]
    psum x1 -> x0, waiting for transfers between devices: 292 us -> none  [shards(): zonal = lax.psum(binned, 'lon')]
    pallas_call x0 -> x1, Pallas kernels: none -> 82.6 us  [overturning(): pl.pallas_call(functools.partial(kernel, comm), in_specs=[hbm] * 4 + [vme...]
    reduce_scatter x2 -> x0, waiting for transfers between devices: 41.9 us -> none  [the longest x1 27.9 us: shards(): lax.psum_scatter(first_sum, 'tm', scatter_dimension=1, tiled=True)]
    div x16 -> x0, other arithmetic: 31.3 us -> none  [one_snapshot(): first = (transport * (weight / 64.0)).reshape(1, -1, rows)]
    sub x17 -> x0, other arithmetic: 22.1 us -> none  [the longest x16 20.9 us: one_snapshot(): relative = (lighter - class_low).reshape(1, -1, rows)]
    mul x16 -> x0, other arithmetic: 13.7 us -> none  [one_snapshot(): first = (transport * (weight / 64.0)).reshape(1, -1, rows)]
  transfers between devices with their start and end apart: 3 -> 0, of which waited for: 3 -> 0; matrix products, arithmetic and copies ran while one was open for 0% -> 0% of each run, Pallas kernels for 0% -> 0%
where the time goes in v1:
time: 89.4 us; the launch traced here: 89.1 us
  Pallas kernels  82.6 us (92%)
  local copies, waits for them, and re-layouts  5.92 us (7%)
    pallas_call x1, Pallas kernels, overturning(): pl.pallas_call(functools.partial(kernel, comm), in_specs=[hbm] * 4 + [vme...  82.6 us
    unnamed x1, local copies, waits for them, and re-layouts  2.96 us
    pallas_call x2, local copies, waits for them, and re-layouts, overturning(): pl.pallas_call(functools.partial(kernel, comm), in_specs=[hbm] * 4 + [vme...  2.96 us

profile of v1, /device:TPU:1, one launch (start us, length us, event | category | flops | bytes accessed | tf_op | source)
XLA Modules:
  0.0 89.1 jit_solution(8926250931993052230)
XLA Ops:
  0.6 82.6 %overturning.1 = (f32[16,120,256]{2,1,0:T(8,128)}, f32[120,4]{1,0:T(8,128)}, f32[120,4]{1,0:T(8,128)}) custom-call(bf16[16,32,32,256]{3,2,1,0:T(8,128)(2,1)} %v_hbm.1, bf16[16,32,32,256]{3,2,1,0:T(8,128)(2,1)} %h_hbm.1, s32[16,32,32,256]{3,2,1,0:T(8,128)} %k_hbm.1, s32[16,32,32,256]{3,2,1,0:T(8,128)} %w_hbm.1, f32[1,256]{1,0:T(1,128)} %bitcast.1), custom_call_target="tpu_custom_call" | custom-call | tf_op jit(solution)/shard_map/overturning/pallas_call | solution.py:412
  83.2 1.5 %copy.8 = f32[120,4]{0,1:T(4,128)} copy(f32[120,4]{1,0:T(8,128)} %get-tuple-element.4) | data formatting | bytes 3840 | tf_op jit(solution)/shard_map/overturning/pallas_call | solution.py:412
  84.7 1.5 %copy.9 = f32[120,4]{0,1:T(4,128)} copy(f32[120,4]{1,0:T(8,128)} %get-tuple-element.5) | data formatting | bytes 3840 | tf_op jit(solution)/shard_map/overturning/pallas_call | solution.py:412
  86.2 3.0 %copy.11 = f32[16,120,256]{2,1,0:T(8,128)} copy(f32[16,120,256]{2,1,0:T(8,128)} %get-tuple-element.9) | data formatting | bytes 3932160

commit v2 on v1

v2 whole, which is shorter than its diff:
```python
import functools
import jax
import jax.numpy as jnp
from jax import lax
from jax.experimental import pallas as pl
from jax.experimental.pallas import tpu as pltpu
from jax.sharding import PartitionSpec as P

C = 240
GROUPS = 8
LAST = 8
NT = (((1,), (1,)), ((), ()))
MESH = pl.DeviceIdType.MESH
F32, BF16 = jnp.float32, jnp.bfloat16


def prepare(raw, turned, chunk):
    lons = pl.ds(chunk * 8, 8)
    cells = pl.ds(pl.multiple_of(chunk * 256, 256), 256)
    speed, layer, lighter, share = (ref[lons].reshape(256, 256) for ref in raw)
    v_t, h_t, hi_t, lo_t, q_t, e_t = turned
    v_t[:, cells] = speed.T
    h_t[:, cells] = layer.T
    k = lighter.astype(F32)
    hi = jnp.floor(k * (1 / 15.0) + (1 / 30.0))
    hi_t[:, cells] = hi.astype(BF16).T
    lo_t[:, cells] = (k - hi * 15.0).astype(BF16).T
    part = layer.astype(F32) * (share.astype(F32) * (1 / 64.0))
    q = part.astype(BF16)
    q_t[:, cells] = q.T
    e_t[:, cells] = (part - q.astype(F32)).astype(BF16).T


def group_sums(turned, rows, diagonal):
    total = None
    for start in range(0, 1024, 256):
        cells = slice(start, start + 256)
        v, h, hi, lo, q, e = (ref[rows, cells] for ref in turned)
        zero = jnp.zeros_like(v)
        a = jnp.concatenate([jnp.where(hi == float(x), v, zero) for x in range(16)], axis=0)
        b, f = [], []
        below = zero
        for x in range(15):
            here = lo == float(x)
            b.append(jnp.where(here, q, below))
            f.append(jnp.where(here, e, zero))
            below = jnp.where(here, h, below)
        b = jnp.concatenate(b + [below], axis=0)
        f = jnp.concatenate(f + [zero], axis=0)
        part = lax.dot_general(
            jnp.concatenate([a, a], axis=1),
            jnp.concatenate([b, f], axis=1),
            NT,
            preferred_element_type=F32,
        )
        total = part if total is None else total + part
    return jnp.where(diagonal[None], total.reshape(16, 16, 256), 0.0).sum(1)


def arrange(sums, width, units, slot_of):
    lane = lax.broadcasted_iota(jnp.int32, (16, 128), 1)
    slot = []
    for part in range(2):
        x = [sums[g, :, part * 128 : part * 128 + 128] for g in range(8)]
        for d in (4, 2, 1):
            high = (lane & (16 * d)) != 0
            y = list(x)
            for i in range(8):
                if i & d == 0:
                    y[i] = jnp.where(high, pltpu.roll(x[i + d], 16 * d, 1), x[i])
                    y[i + d] = jnp.where(high, x[i + d], pltpu.roll(x[i], 128 - 16 * d, 1))
            x = y
        slot += x
    hi = lax.broadcasted_iota(jnp.int32, (16, 128), 0)
    run = slot[15]
    for d in (1, 2, 4, 8):
        run = run + jnp.where(hi >= d, pltpu.roll(run, d, 0), 0.0)
    offset = run - slot[15]
    for x in range(15):
        y = (slot[x] + offset) * width
        for cut in range(2):
            units[slot_of(cut), pl.ds(x, 8, stride=15), :] = y[cut * 8 : cut * 8 + 8]


def kernel(comm, v_hbm, h_hbm, k_hbm, w_hbm, width, psi_hbm, mean_ref, var_ref, *scratch):
    (raw_v, raw_h, raw_k, raw_w), scratch = scratch[:4], scratch[4:]
    even, odd, scratch = scratch[:6], scratch[6:12], scratch[12:]
    (sums, send, got_1, mid, got_2, own, pad, stat, got_3, read_sem, write_sem) = scratch[:11]
    (s1, r1, s2, r2, s3, r3, s4, r4, s5, r5) = scratch[11:]
    if comm:
        tm, lon, cls = lax.axis_index("tm"), lax.axis_index("lon"), lax.axis_index("cls")
    else:
        tm, lon, cls = jnp.int32(0), jnp.int32(0), jnp.int32(0)
    zz, xx, yy = lon // 8, (lon // 2) % 4, lon % 2
    n_own = 8

    def read(s, slot):
        return [
            pltpu.make_async_copy(src.at[cls * n_own + s], dst.at[slot], read_sem.at[slot, i])
            for i, (src, dst) in enumerate(
                zip((v_hbm, h_hbm, k_hbm, w_hbm), (raw_v, raw_h, raw_k, raw_w))
            )
        ]

    spots = ((xx, zz), (zz, xx))
    cols, col_lon, place, place_lon = [], [], [], []
    for p, (a, b) in enumerate(spots):
        step_a, step_b = (8, 2) if p else (2, 8)
        near = [a] + [(a + rel) % 4 for rel in (1, 2, 3)]
        cols.append(near)
        col_lon.append([c * step_a + b * step_b + yy for c in near])
        me = b * 2 + yy
        near = [me] + [(me + rel) % 8 for rel in range(1, 8)]
        place.append(near)
        place_lon.append([a * step_a + (n // 2) * step_b + n % 2 for n in near])
    home = [(cls + a // 2) % 2 for a, _ in spots]

    def size(job):
        return 128 if job[3] is None else 64

    def unit_of(job, col):
        half = job[3]
        if half is None:
            return col, 0, col % 2
        return (col // 2) * 2 + half, (col % 2) * 64, half

    def base(job, n):
        return 0 if job[3] is None else job[3] * n

    def span(start, n):
        return pl.ds(start if isinstance(start, int) else pl.multiple_of(start, 8), n)

    def first(job, rel):
        i, p, s, _ = job
        n = size(job)
        u, r, _ = unit_of(job, cols[p][rel])
        return pltpu.make_async_remote_copy(
            src_ref=send.at[s, u, span(r, n)], dst_ref=got_1.at[s, 3 - rel, span(base(job, 64), n)],
            send_sem=s1.at[i, rel - 1], recv_sem=r1.at[i, 3 - rel],
            device_id={"lon": col_lon[p][rel]}, device_id_type=MESH)

    def second(job, rel):
        i, p, s, _ = job
        n = size(job) // 8
        return pltpu.make_async_remote_copy(
            src_ref=mid.at[s, span(base(job, 64) + place[p][rel] * n, n)],
            dst_ref=got_2.at[s, 7 - rel, span(base(job, 8), n)],
            send_sem=s2.at[i, rel - 1], recv_sem=r2.at[i, 7 - rel],
            device_id={"lon": place_lon[p][rel]}, device_id_type=MESH)

    def target(job, group, rel):
        _, p, s, _ = job
        n = size(job) // 8
        _, r, half = unit_of(job, cols[p][0])
        return pad.at[group * n_own + s, half, span(r + place[p][rel] * n, n)]

    def third(job, rel):
        i, p, s, _ = job
        return pltpu.make_async_remote_copy(
            src_ref=own.at[s, span(base(job, 8), size(job) // 8)], dst_ref=target(job, cls, 0),
            send_sem=s3.at[i, rel], recv_sem=r3.at[i, (8 - rel) % 8],
            device_id={"lon": place_lon[p][rel], "cls": home[p]}, device_id_type=MESH)

    def third_got(job, rel):
        i, p, s, _ = job
        return pltpu.make_async_remote_copy(
            src_ref=own.at[s, span(base(job, 8), size(job) // 8)], dst_ref=target(job, home[p], rel),
            send_sem=s3.at[i, rel], recv_sem=r3.at[i, rel],
            device_id={"lon": place_lon[p][rel], "cls": home[p]}, device_id_type=MESH)

    def spread(job, rel):
        _, p, s, _ = job
        col = cols[p][rel]
        _, r, half = unit_of(job, col)
        return pad.at[(cls + col // 2) % 2 * n_own + s, half, span(r, size(job))]

    def fourth(job, rel):
        i, p, _, _ = job
        return pltpu.make_async_remote_copy(
            src_ref=spread(job, 0), dst_ref=spread(job, 0), send_sem=s4.at[i, rel - 1],
            recv_sem=r4.at[i, 3 - rel], device_id={"lon": col_lon[p][rel]}, device_id_type=MESH)

    def fourth_got(job, rel):
        i, p, _, _ = job
        dst = spread(job, rel)
        return pltpu.make_async_remote_copy(
            src_ref=dst, dst_ref=dst, send_sem=s4.at[i, rel - 1], recv_sem=r4.at[i, rel - 1],
            device_id={"lon": col_lon[p][rel]}, device_id_type=MESH)

    def write(s):
        return [
            pltpu.make_async_copy(
                pad.at[base + s, half, pl.ds(0, C // 2)],
                psi_hbm.at[base + s, :, pl.ds(half * 128, 128)],
                write_sem.at[s, base // 4 + half])
            for base in (0, n_own) for half in (0, 1)
        ]

    def start_1(job):
        for rel in (1, 2, 3):
            first(job, rel).start()

    def start_2(job):
        _, p, s, _ = job
        n = size(job)
        u, r, _ = unit_of(job, cols[p][0])
        rows = span(base(job, 64), n)
        for rel in (1, 2, 3):
            first(job, rel).wait_recv()
        mid[s, rows] = send[s, u, span(r, n)] + got_1[s, 0, rows] + got_1[s, 1, rows] + got_1[s, 2, rows]
        for rel in range(1, 8):
            second(job, rel).start()

    def start_3(job):
        _, p, s, _ = job
        n = size(job) // 8
        rows = span(base(job, 8), n)
        for rel in range(1, 8):
            second(job, rel).wait_recv()
        total = mid[s, span(base(job, 64) + place[p][0] * n, n)]
        for i in range(7):
            total = total + got_2[s, i, rows]
        own[s, rows] = total

        @pl.when(cols[p][0] < 2)
        def _():
            target(job, cls, 0)[...] = total

        @pl.when(cols[p][0] >= 2)
        def _():
            third(job, 0).start()

        for rel in range(1, 8):
            third(job, rel).start()

    def start_4(job):
        p = job[1]

        @pl.when(cols[p][0] >= 2)
        def _():
            third_got(job, 0).wait_recv()

        for rel in range(1, 8):
            third_got(job, rel).wait_recv()
        for rel in (1, 2, 3):
            fourth(job, rel).start()

    def take(s):
        for half in range(2):
            one, two = stat[half, 0], stat[half, 1]
            for base in (0, n_own):
                x = pad[base + s, half]
                one = one + x
                two = two + x * x
            stat[half, 0] = one
            stat[half, 1] = two

    def finish(job):
        for rel in (1, 2, 3):
            fourth_got(job, rel).wait_recv()
        if job[0] is not LAST - 1:
            for copy in write(job[2]):
                copy.start()
            take(job[2])

    def drain(job):
        for rel in (1, 2, 3):
            first(job, rel).wait_send()
            fourth(job, rel).wait_send()
        for rel in range(1, 8):
            second(job, rel).wait_send()
            third(job, rel).wait_send()

        @pl.when(cols[job[1]][0] >= 2)
        def _():
            third(job, 0).wait_send()

        if job[0] is not LAST - 1:
            for copy in write(job[2]):
                copy.wait()

    def whole(q, s):
        return (s, q, s, None)

    ends = ((LAST - 1, 1, 7, 0), (LAST, 0, 7, 1))

    barrier = None
    if comm:
        barrier = pltpu.get_barrier_semaphore()
        def greet(to, where):
            pl.semaphore_signal(barrier, inc=1, device_id=where, device_id_type=MESH)

        for y in range(2):
            for i in range(4):
                for near in range(2):
                    group = (cls + near) % 2
                    row = {"lon": ((zz + i) % 4) * 8 + xx * 2 + (yy + y) % 2, "cls": group}
                    if near or i or y:
                        greet(None, row)
                    if i:
                        greet(None, {"lon": zz * 8 + ((xx + i) % 4) * 2 + (yy + y) % 2, "cls": group})
        greet(None, {"tm": 1 - tm})
    n_greet = 2 * 2 * 4 - 1 + 2 * 2 * 3 + 1

    lane = lax.broadcasted_iota(jnp.int32, (16, 256), 1)
    row = lax.broadcasted_iota(jnp.int32, (16, 256), 0)
    diagonal = (lane & 15) == row
    raws = [[ref.at[slot] for ref in (raw_v, raw_h, raw_k, raw_w)] for slot in range(2)]

    for copy in read(0, 0):
        copy.start()
    for copy in read(1, 1):
        copy.start()
    stat[...] = jnp.zeros_like(stat)
    for copy in read(0, 0):
        copy.wait()

    def pad_rows(s, carry):
        for u in range(4):
            send[s, u, pl.ds(C // 2, 8), :] = jnp.zeros((8, 128), F32)
        return carry

    lax.fori_loop(0, n_own, pad_rows, 0)

    def prologue(chunk, carry):
        prepare(raws[0], even, chunk)
        return carry

    lax.fori_loop(0, 4, prologue, 0)

    def compute(s, p):
        here, there = (odd, even) if p else (even, odd)

        @pl.when(s + 2 < n_own)
        def _():
            for copy in read(s + 2, p):
                copy.start()

        @pl.when(s + 1 < n_own)
        def _():
            for copy in read(s + 1, 1 - p):
                copy.wait()

        def step(j, carry):
            for c in range(GROUPS // 4):
                prepare(raws[1 - p], there, j * (GROUPS // 4) + c)
            for g in range(GROUPS):
                rows = pl.ds(pl.multiple_of((j * GROUPS + g) * 16, 16), 16)
                sums[g] = group_sums(here, rows, diagonal)
            arrange(sums, width[pl.ds(j, 1), :], send.at[s], lambda cut: ((cls + cut) % 2) * 2 + j)
            if comm and p == 1:
                @pl.when((s == n_own - 1) & (j == 0))
                def _():
                    start_1(ends[0])
                    start_2(whole(0, 6))
                    start_3(whole(1, 5))
                    start_4(whole(0, 4))
                    finish(whole(1, 3))
            return carry

        lax.fori_loop(0, 16 // GROUPS, step, 0)

    def pair(t, carry):
        for p in range(2):
            s = 2 * t + p
            compute(s, p)
            if not comm:
                continue

            def advance():
                start_1(whole(p, s))
                for least, go, q in ((1, start_2, 1 - p), (2, start_3, p), (3, start_4, 1 - p), (4, finish, p)):
                    if least <= p:
                        go(whole(q, s - least))
                    else:
                        @pl.when(s >= least)
                        def _(go=go, q=q, least=least):
                            go(whole(q, s - least))

            if p == 0:
                @pl.when(t == 0)
                def _():
                    pl.semaphore_wait(barrier, n_greet)
                advance()
            else:
                pl.when(s < n_own - 1)(advance)
        return carry

    lax.fori_loop(0, n_own // 2, pair, 0)
    if comm:
        early, late = ends
        start_1(late)
        start_2(early)
        start_3(whole(0, 6))
        start_4(whole(1, 5))
        finish(whole(0, 4))
        start_2(late)
        start_3(early)
        start_4(whole(0, 6))
        finish(whole(1, 5))
        start_3(late)
        start_4(early)
        finish(whole(0, 6))
        start_4(late)
        finish(early)
        finish(late)
        swap = pltpu.make_async_remote_copy(
            src_ref=stat.at[1 - tm], dst_ref=got_3, send_sem=s5, recv_sem=r5,
            device_id={"tm": 1 - tm}, device_id_type=MESH)
        swap.start()

        def drains(t, carry):
            drain(whole(0, 2 * t))
            drain(whole(1, 2 * t + 1))
            return carry

        lax.fori_loop(0, n_own // 2 - 1, drains, 0)
        drain(whole(0, 6))
        for job in ends:
            drain(job)
        swap.wait()
    else:
        for s in range(8):
            pad[s, 0] = send[s, 0]
            pad[s, 1] = send[s, 1]
            pad[s + 8, 0] = send[s, 2]
            pad[s + 8, 1] = send[s, 3]
        for s in (0, 7):
            for copy in write(s):
                copy.start()
            for copy in write(s):
                copy.wait()
        got_3[...] = jnp.zeros_like(got_3)
    count = 32.0
    mean = (stat[tm, 0] + got_3[0]) / count
    var = (stat[tm, 1] + got_3[1]) / count - mean * mean
    mean_ref[...] = pltpu.roll(mean, (128 - lon * 4) % 128, 1)[: C // 2, :4]
    var_ref[...] = pltpu.roll(var, (128 - lon * 4) % 128, 1)[: C // 2, :4]


def overturning(v, h, k, w, width, comm=True):
    dma = pltpu.SemaphoreType.DMA
    hbm = pl.BlockSpec(memory_space=pl.ANY)
    vmem = pl.BlockSpec(memory_space=pltpu.VMEM)
    scratch = [pltpu.VMEM((2, 32, 32, 256), d) for d in (BF16, BF16, jnp.int32, jnp.int32)]
    scratch += [pltpu.VMEM((256, 1024), BF16)] * 12
    scratch += [
        pltpu.VMEM((GROUPS, 16, 256), F32),
        pltpu.VMEM((8, 4, 128, 128), F32),
        pltpu.VMEM((8, 3, 128, 128), F32),
        pltpu.VMEM((8, 128, 128), F32),
        pltpu.VMEM((8, 7, 16, 128), F32),
        pltpu.VMEM((8, 16, 128), F32),
        pltpu.VMEM((16, 2, 128, 128), F32),
        pltpu.VMEM((2, 2, 128, 128), F32),
        pltpu.VMEM((2, 128, 128), F32),
        dma((2, 4)), dma((8, 4)),
        dma((9, 3)), dma((9, 3)), dma((9, 7)), dma((9, 7)),
        dma((9, 8)), dma((9, 8)), dma((9, 3)), dma((9, 3)), dma, dma,
    ]
    return pl.pallas_call(
        functools.partial(kernel, comm),
        in_specs=[hbm] * 4 + [vmem],
        out_specs=(hbm, vmem, vmem),
        out_shape=(
            jax.ShapeDtypeStruct((16, C // 2, 256), F32),
            jax.ShapeDtypeStruct((C // 2, 4), F32),
            jax.ShapeDtypeStruct((C // 2, 4), F32),
        ),
        scratch_shapes=scratch,
        compiler_params=pltpu.CompilerParams(
            vmem_limit_bytes=56 * 2**20,
            **(dict(collective_id=0, has_side_effects=True) if comm else {}),
        ),
        name="overturning",
    )(v, h, k, w, width)


def shards(velocity, thickness, class_index, layer_weight, zonal_width):
    return overturning(velocity, thickness, class_index, layer_weight, zonal_width.reshape(2, -1))


def solution(mesh):
    cells = P("tm", "lon", None, None)
    in_specs = (cells, cells, cells, cells, P())
    out_specs = (P("tm", "cls", None), P("cls", ("tm", "lon")), P("cls", ("tm", "lon")))
    return jax.shard_map(shards, mesh=mesh, in_specs=in_specs, out_specs=out_specs, check_vma=False)
```

time: 89.4 us -> 93 us (1.040)
  Pallas kernels: 82.6 us -> 86.2 us
    pallas_call x1, Pallas kernels: 82.6 us -> 86.2 us  [overturning(): pl.pallas_call(functools.partial(kernel, comm), in_specs=[hbm] * 4 + [vme...]
where the time goes in v2:
time: 93 us; the launch traced here: 92.7 us
  Pallas kernels  86.2 us (93%)
  local copies, waits for them, and re-layouts  5.92 us (6%)
    pallas_call x1, Pallas kernels, overturning(): pl.pallas_call(functools.partial(kernel, comm), in_specs=[hbm] * 4 + [vme...  86.2 us
    unnamed x1, local copies, waits for them, and re-layouts  2.96 us
    pallas_call x2, local copies, waits for them, and re-layouts, overturning(): pl.pallas_call(functools.partial(kernel, comm), in_specs=[hbm] * 4 + [vme...  2.96 us

profile of v2, /device:TPU:1, one launch (start us, length us, event | category | flops | bytes accessed | tf_op | source)
XLA Modules:
  0.0 92.7 jit_solution(13681373362587760721)
XLA Ops:
  0.6 86.2 %overturning.1 = (f32[16,120,256]{2,1,0:T(8,128)}, f32[120,4]{1,0:T(8,128)}, f32[120,4]{1,0:T(8,128)}) custom-call(bf16[16,32,32,256]{3,2,1,0:T(8,128)(2,1)} %v_hbm.1, bf16[16,32,32,256]{3,2,1,0:T(8,128)(2,1)} %h_hbm.1, s32[16,32,32,256]{3,2,1,0:T(8,128)} %k_hbm.1, s32[16,32,32,256]{3,2,1,0:T(8,128)} %w_hbm.1, f32[2,128]{1,0:T(2,128)} %bitcast.1), custom_call_target="tpu_custom_call" | custom-call | tf_op jit(solution)/shard_map/overturning/pallas_call | solution.py:461
  86.8 1.5 %copy.8 = f32[120,4]{0,1:T(4,128)} copy(f32[120,4]{1,0:T(8,128)} %get-tuple-element.4) | data formatting | bytes 3840 | tf_op jit(solution)/shard_map/overturning/pallas_call | solution.py:461
  88.3 1.5 %copy.9 = f32[120,4]{0,1:T(4,128)} copy(f32[120,4]{1,0:T(8,128)} %get-tuple-element.5) | data formatting | bytes 3840 | tf_op jit(solution)/shard_map/overturning/pallas_call | solution.py:461
  89.8 3.0 %copy.11 = f32[16,120,256]{2,1,0:T(8,128)} copy(f32[16,120,256]{2,1,0:T(8,128)} %get-tuple-element.9) | data formatting | bytes 3932160

commit v3 on v2

--- a/solution.py
+++ b/solution.py
@@ -20,12 +20,12 @@
     speed, layer, lighter, share = (ref[lons].reshape(256, 256) for ref in raw)
     v_t, h_t, hi_t, lo_t, q_t, e_t = turned
     v_t[:, cells] = speed.T
-    h_t[:, cells] = layer.T
+    h_t[:, cells] = (layer * 64.0).T
     k = lighter.astype(F32)
-    hi = jnp.floor(k * (1 / 15.0) + (1 / 30.0))
-    hi_t[:, cells] = hi.astype(BF16).T
-    lo_t[:, cells] = (k - hi * 15.0).astype(BF16).T
-    part = layer.astype(F32) * (share.astype(F32) * (1 / 64.0))
+    hi = (k * (1 / 15.0) + (129 - 7 / 15.0)).astype(BF16)
+    hi_t[:, cells] = hi.T
+    lo_t[:, cells] = (k.astype(BF16) - (hi - 129.0) * 15.0).T
+    part = layer.astype(F32) * share.astype(F32)
     q = part.astype(BF16)
     q_t[:, cells] = q.T
     e_t[:, cells] = (part - q.astype(F32)).astype(BF16).T
@@ -37,7 +37,7 @@
         cells = slice(start, start + 256)
         v, h, hi, lo, q, e = (ref[rows, cells] for ref in turned)
         zero = jnp.zeros_like(v)
-        a = jnp.concatenate([jnp.where(hi == float(x), v, zero) for x in range(16)], axis=0)
+        a = jnp.concatenate([jnp.where(hi == float(x + 129), v, zero) for x in range(16)], axis=0)
         b, f = [], []
         below = zero
         for x in range(15):
@@ -48,18 +48,16 @@
         b = jnp.concatenate(b + [below], axis=0)
         f = jnp.concatenate(f + [zero], axis=0)
         part = lax.dot_general(
-            jnp.concatenate([a, a], axis=1),
-            jnp.concatenate([b, f], axis=1),
-            NT,
-            preferred_element_type=F32,
+            jnp.concatenate([b, f], axis=0), a, NT, preferred_element_type=F32
         )
         total = part if total is None else total + part
+    total = total[:256] + total[256:]
     return jnp.where(diagonal[None], total.reshape(16, 16, 256), 0.0).sum(1)
 
 
 def arrange(sums, width, units, slot_of):
     lane = lax.broadcasted_iota(jnp.int32, (16, 128), 1)
-    slot = []
+    offset = jnp.zeros((1, 128), F32)
     for part in range(2):
         x = [sums[g, :, part * 128 : part * 128 + 128] for g in range(8)]
         for d in (4, 2, 1):
@@ -70,23 +68,16 @@
                     y[i] = jnp.where(high, pltpu.roll(x[i + d], 16 * d, 1), x[i])
                     y[i + d] = jnp.where(high, x[i + d], pltpu.roll(x[i], 128 - 16 * d, 1))
             x = y
-        slot += x
-    hi = lax.broadcasted_iota(jnp.int32, (16, 128), 0)
-    run = slot[15]
-    for d in (1, 2, 4, 8):
-        run = run + jnp.where(hi >= d, pltpu.roll(run, d, 0), 0.0)
-    offset = run - slot[15]
-    for x in range(15):
-        y = (slot[x] + offset) * width
-        for cut in range(2):
-            units[slot_of(cut), pl.ds(x, 8, stride=15), :] = y[cut * 8 : cut * 8 + 8]
-
-
-def kernel(comm, v_hbm, h_hbm, k_hbm, w_hbm, width, psi_hbm, mean_ref, var_ref, *scratch):
+        for i in range(8):
+            units[slot_of(part), 15 * i : 15 * i + 16, :] = (x[i] + offset) * width
+            offset = offset + x[i][15:16]
+
+
+def kernel(comm, v_hbm, h_hbm, k_hbm, w_hbm, width, psi_hbm, total_ref, *scratch):
     (raw_v, raw_h, raw_k, raw_w), scratch = scratch[:4], scratch[4:]
     even, odd, scratch = scratch[:6], scratch[6:12], scratch[12:]
-    (sums, send, got_1, mid, got_2, own, pad, stat, got_3, read_sem, write_sem) = scratch[:11]
-    (s1, r1, s2, r2, s3, r3, s4, r4, s5, r5) = scratch[11:]
+    (sums, send, got_1, mid, got_2, own, pad, stat, got_3, read_sem, quarter_sem, write_sem) = scratch[:12]
+    (s1, r1, s2, r2, s3, r3, s4, r4, s5, r5) = scratch[12:]
     if comm:
         tm, lon, cls = lax.axis_index("tm"), lax.axis_index("lon"), lax.axis_index("cls")
     else:
@@ -120,9 +111,7 @@
 
     def unit_of(job, col):
         half = job[3]
-        if half is None:
-            return col, 0, col % 2
-        return (col // 2) * 2 + half, (col % 2) * 64, half
+        return col, 0 if half is None else half * 64, col % 2
 
     def base(job, n):
         return 0 if job[3] is None else job[3] * n
@@ -190,8 +179,8 @@
     def write(s):
         return [
             pltpu.make_async_copy(
-                pad.at[base + s, half, pl.ds(0, C // 2)],
-                psi_hbm.at[base + s, :, pl.ds(half * 128, 128)],
+                pad.at[base + s, half],
+                psi_hbm.at[base + s, half],
                 write_sem.at[s, base // 4 + half])
             for base in (0, n_own) for half in (0, 1)
         ]
@@ -307,14 +296,21 @@
     diagonal = (lane & 15) == row
     raws = [[ref.at[slot] for ref in (raw_v, raw_h, raw_k, raw_w)] for slot in range(2)]
 
-    for copy in read(0, 0):
-        copy.start()
+    def quarter(chunk):
+        lons = pl.ds(chunk * 8, 8)
+        return [
+            pltpu.make_async_copy(src.at[cls * n_own, lons], dst.at[0, lons], quarter_sem.at[chunk, i])
+            for i, (src, dst) in enumerate(
+                zip((v_hbm, h_hbm, k_hbm, w_hbm), (raw_v, raw_h, raw_k, raw_w))
+            )
+        ]
+
+    for chunk in range(4):
+        for copy in quarter(chunk):
+            copy.start()
     for copy in read(1, 1):
         copy.start()
     stat[...] = jnp.zeros_like(stat)
-    for copy in read(0, 0):
-        copy.wait()
-
     def pad_rows(s, carry):
         for u in range(4):
             send[s, u, pl.ds(C // 2, 8), :] = jnp.zeros((8, 128), F32)
@@ -323,6 +319,8 @@
     lax.fori_loop(0, n_own, pad_rows, 0)
 
     def prologue(chunk, carry):
+        for copy in quarter(chunk):
+            copy.wait()
         prepare(raws[0], even, chunk)
         return carry
 
@@ -346,19 +344,12 @@
                 prepare(raws[1 - p], there, j * (GROUPS // 4) + c)
             for g in range(GROUPS):
                 rows = pl.ds(pl.multiple_of((j * GROUPS + g) * 16, 16), 16)
-                sums[g] = group_sums(here, rows, diagonal)
-            arrange(sums, width[pl.ds(j, 1), :], send.at[s], lambda cut: ((cls + cut) % 2) * 2 + j)
-            if comm and p == 1:
-                @pl.when((s == n_own - 1) & (j == 0))
-                def _():
-                    start_1(ends[0])
-                    start_2(whole(0, 6))
-                    start_3(whole(1, 5))
-                    start_4(whole(0, 4))
-                    finish(whole(1, 3))
+                sums[j * GROUPS + g] = group_sums(here, rows, diagonal)
             return carry
 
         lax.fori_loop(0, 16 // GROUPS, step, 0)
+        for j in range(2):
+            arrange(sums.at[pl.ds(j * 8, 8)], width[j : j + 1, :], send.at[s], lambda cut: ((cls + cut) % 2) * 2 + j)
 
     def pair(t, carry):
         for p in range(2):
@@ -388,22 +379,26 @@
 
     lax.fori_loop(0, n_own // 2, pair, 0)
     if comm:
-        early, late = ends
-        start_1(late)
-        start_2(early)
+        for job in ends:
+            start_1(job)
+        start_2(whole(0, 6))
+        start_3(whole(1, 5))
+        start_4(whole(0, 4))
+        finish(whole(1, 3))
+        for job in ends:
+            start_2(job)
         start_3(whole(0, 6))
         start_4(whole(1, 5))
         finish(whole(0, 4))
-        start_2(late)
-        start_3(early)
+        for job in ends:
+            start_3(job)
         start_4(whole(0, 6))
         finish(whole(1, 5))
-        start_3(late)
-        start_4(early)
+        for job in ends:
+            start_4(job)
         finish(whole(0, 6))
-        start_4(late)
-        finish(early)
-        finish(late)
+        for job in ends:
+            finish(job)
         swap = pltpu.make_async_remote_copy(
             src_ref=stat.at[1 - tm], dst_ref=got_3, send_sem=s5, recv_sem=r5,
             device_id={"tm": 1 - tm}, device_id_type=MESH)
@@ -431,11 +426,26 @@
             for copy in write(s):
                 copy.wait()
         got_3[...] = jnp.zeros_like(got_3)
-    count = 32.0
-    mean = (stat[tm, 0] + got_3[0]) / count
-    var = (stat[tm, 1] + got_3[1]) / count - mean * mean
-    mean_ref[...] = pltpu.roll(mean, (128 - lon * 4) % 128, 1)[: C // 2, :4]
-    var_ref[...] = pltpu.roll(var, (128 - lon * 4) % 128, 1)[: C // 2, :4]
+    total_ref[...] = stat[tm] + got_3[...]
+
+
+def finals(pad_hbm, total, psi_hbm, mean_ref, var_ref, sem):
+    copies = [
+        pltpu.make_async_copy(
+            pad_hbm.at[s, half, pl.ds(0, C // 2)], psi_hbm.at[s, :, pl.ds(half * 128, 128)], sem.at[s, half]
+        )
+        for s in range(16)
+        for half in range(2)
+    ]
+    for copy in copies:
+        copy.start()
+    mean = total[0] / 32.0
+    var = total[1] / 32.0 - mean * mean
+    shift = (128 - lax.axis_index("lon") * 4) % 128
+    mean_ref[...] = pltpu.roll(mean, shift, 1).T[:4, : C // 2]
+    var_ref[...] = pltpu.roll(var, shift, 1).T[:4, : C // 2]
+    for copy in copies:
+        copy.wait()
 
 
 def overturning(v, h, k, w, width, comm=True):
@@ -445,7 +455,7 @@
     scratch = [pltpu.VMEM((2, 32, 32, 256), d) for d in (BF16, BF16, jnp.int32, jnp.int32)]
     scratch += [pltpu.VMEM((256, 1024), BF16)] * 12
     scratch += [
-        pltpu.VMEM((GROUPS, 16, 256), F32),
+        pltpu.VMEM((16, 16, 256), F32),
         pltpu.VMEM((8, 4, 128, 128), F32),
         pltpu.VMEM((8, 3, 128, 128), F32),
         pltpu.VMEM((8, 128, 128), F32),
@@ -454,18 +464,17 @@
         pltpu.VMEM((16, 2, 128, 128), F32),
         pltpu.VMEM((2, 2, 128, 128), F32),
         pltpu.VMEM((2, 128, 128), F32),
-        dma((2, 4)), dma((8, 4)),
+        dma((2, 4)), dma((4, 4)), dma((8, 4)),
         dma((9, 3)), dma((9, 3)), dma((9, 7)), dma((9, 7)),
         dma((9, 8)), dma((9, 8)), dma((9, 3)), dma((9, 3)), dma, dma,
     ]
     return pl.pallas_call(
         functools.partial(kernel, comm),
         in_specs=[hbm] * 4 + [vmem],
-        out_specs=(hbm, vmem, vmem),
+        out_specs=(hbm, vmem),
         out_shape=(
-            jax.ShapeDtypeStruct((16, C // 2, 256), F32),
-            jax.ShapeDtypeStruct((C // 2, 4), F32),
-            jax.ShapeDtypeStruct((C // 2, 4), F32),
+            jax.ShapeDtypeStruct((16, 2, 128, 128), F32),
+            jax.ShapeDtypeStruct((2, 128, 128), F32),
         ),
         scratch_shapes=scratch,
         compiler_params=pltpu.CompilerParams(
@@ -477,7 +486,23 @@
 
 
 def shards(velocity, thickness, class_index, layer_weight, zonal_width):
-    return overturning(velocity, thickness, class_index, layer_weight, zonal_width.reshape(2, -1))
+    pad, total = overturning(velocity, thickness, class_index, layer_weight, zonal_width.reshape(2, -1) * (1 / 64.0))
+    hbm = pl.BlockSpec(memory_space=pl.ANY)
+    vmem = pl.BlockSpec(memory_space=pltpu.VMEM)
+    psi, mean, var = pl.pallas_call(
+        finals,
+        in_specs=[hbm, vmem],
+        out_specs=(hbm, vmem, vmem),
+        out_shape=(
+            jax.ShapeDtypeStruct((16, C // 2, 256), F32),
+            jax.ShapeDtypeStruct((4, C // 2), F32),
+            jax.ShapeDtypeStruct((4, C // 2), F32),
+        ),
+        scratch_shapes=[pltpu.SemaphoreType.DMA((16, 2))],
+        compiler_params=pltpu.CompilerParams(vmem_limit_bytes=60 * 2**20),
+        name="finals",
+    )(pad, total)
+    return psi, mean.T, var.T
 
 
 def solution(mesh):

time: 93 us -> 144 us (1.55)
  Pallas kernels: 86.2 us -> 142 us
  local copies, waits for them, and re-layouts: 5.92 us -> 0 us
    pallas_call x0 -> x1, Pallas kernels: none -> 62.4 us  [shards(): pl.pallas_call(finals, in_specs=[hbm, vmem], out_specs=(hbm, vmem, vmem),...]
    pallas_call x1, Pallas kernels: 86.2 us -> 79.9 us  [overturning(): pl.pallas_call(functools.partial(kernel, comm), in_specs=[hbm] * 4 + [vme...]
    unnamed x1 -> x0, local copies, waits for them, and re-layouts: 2.96 us -> none
    pallas_call x2 -> x0, local copies, waits for them, and re-layouts: 2.96 us -> none  [overturning(): pl.pallas_call(functools.partial(kernel, comm), in_specs=[hbm] * 4 + [vme...]
where the time goes in v3:
time: 144 us
  Pallas kernels  142 us (99%)
    pallas_call x1, Pallas kernels, overturning(): pl.pallas_call(functools.partial(kernel, comm), in_specs=[hbm] * 4 + [vme...  79.9 us
    pallas_call x1, Pallas kernels, shards(): pl.pallas_call(finals, in_specs=[hbm, vmem], out_specs=(hbm, vmem, vmem),...  62.4 us

profile of v3, /device:TPU:1, one launch (start us, length us, event | category | flops | bytes accessed | tf_op | source)
XLA Modules:
  0.0 144.2 jit_solution(987620274986153671)
XLA Ops:
  0.6 1.2 multiply_bitcast_fusion.width
  1.9 79.9 %overturning.1 = (f32[16,2,128,128]{3,2,1,0:T(8,128)}, f32[2,128,128]{2,1,0:T(8,128)}) custom-call(bf16[16,32,32,256]{3,2,1,0:T(8,128)(2,1)} %v_hbm.1, bf16[16,32,32,256]{3,2,1,0:T(8,128)(2,1)} %h_hbm.1, s32[16,32,32,256]{3,2,1,0:T(8,128)} %k_hbm.1, s32[16,32,32,256]{3,2,1,0:T(8,128)} %w_hbm.1, f32[2,128]{1,0:T(2,128)} %multiply_bitcast_fusion.width), custom_call_target="tpu_custom_call" | custom-call | tf_op jit(solution)/shard_map/overturning/pallas_call | solution.py:471
  81.7 62.4 %finals.1 = (f32[16,120,256]{2,1,0:T(8,128)}, f32[4,120]{1,0:T(4,128)}, f32[4,120]{1,0:T(4,128)}) custom-call(f32[16,2,128,128]{3,2,1,0:T(8,128)} %get-tuple-element.8.pad_hbm, f32[2,128,128]{2,1,0:T(8,128)} %get-tuple-element.9.total), custom_call_target="tpu_custom_call" | custom-call | tf_op jit(solution)/shard_map/finals/pallas_call | solution.py:492

commit v4 on v3

--- a/solution.py
+++ b/solution.py
@@ -349,7 +349,7 @@
 
         lax.fori_loop(0, 16 // GROUPS, step, 0)
         for j in range(2):
-            arrange(sums.at[pl.ds(j * 8, 8)], width[j : j + 1, :], send.at[s], lambda cut: ((cls + cut) % 2) * 2 + j)
+            arrange(sums.at[pl.ds(j * 8, 8)], width[j : j + 1, :] * (1 / 64.0), send.at[s], lambda cut: ((cls + cut) % 2) * 2 + j)
 
     def pair(t, carry):
         for p in range(2):
@@ -429,22 +429,30 @@
     total_ref[...] = stat[tm] + got_3[...]
 
 
-def finals(pad_hbm, total, psi_hbm, mean_ref, var_ref, sem):
-    copies = [
+def finals(pad_hbm, total, psi_hbm, mean_ref, var_ref, pad, read_sem, sem):
+    reads = [
+        pltpu.make_async_copy(pad_hbm.at[pl.ds(4 * i, 4)], pad.at[pl.ds(4 * i, 4)], read_sem.at[i])
+        for i in range(4)
+    ]
+    writes = [
         pltpu.make_async_copy(
-            pad_hbm.at[s, half, pl.ds(0, C // 2)], psi_hbm.at[s, :, pl.ds(half * 128, 128)], sem.at[s, half]
+            pad.at[s, half, pl.ds(0, C // 2)], psi_hbm.at[s, :, pl.ds(half * 128, 128)], sem.at[s, half]
         )
         for s in range(16)
         for half in range(2)
     ]
-    for copy in copies:
+    for copy in reads:
         copy.start()
     mean = total[0] / 32.0
     var = total[1] / 32.0 - mean * mean
     shift = (128 - lax.axis_index("lon") * 4) % 128
     mean_ref[...] = pltpu.roll(mean, shift, 1).T[:4, : C // 2]
     var_ref[...] = pltpu.roll(var, shift, 1).T[:4, : C // 2]
-    for copy in copies:
+    for i in range(4):
+        reads[i].wait()
+        for copy in writes[8 * i : 8 * i + 8]:
+            copy.start()
+    for copy in writes:
         copy.wait()
 
 
@@ -486,7 +494,7 @@
 
 
 def shards(velocity, thickness, class_index, layer_weight, zonal_width):
-    pad, total = overturning(velocity, thickness, class_index, layer_weight, zonal_width.reshape(2, -1) * (1 / 64.0))
+    pad, total = overturning(velocity, thickness, class_index, layer_weight, zonal_width.reshape(2, -1))
     hbm = pl.BlockSpec(memory_space=pl.ANY)
     vmem = pl.BlockSpec(memory_space=pltpu.VMEM)
     psi, mean, var = pl.pallas_call(
@@ -498,7 +506,11 @@
             jax.ShapeDtypeStruct((4, C // 2), F32),
             jax.ShapeDtypeStruct((4, C // 2), F32),
         ),
-        scratch_shapes=[pltpu.SemaphoreType.DMA((16, 2))],
+        scratch_shapes=[
+            pltpu.VMEM((16, 2, 128, 128), F32),
+            pltpu.SemaphoreType.DMA((4,)),
+            pltpu.SemaphoreType.DMA((16, 2)),
+        ],
         compiler_params=pltpu.CompilerParams(vmem_limit_bytes=60 * 2**20),
         name="finals",
     )(pad, total)

time: 144 us -> 84.6 us (0.59)
  Pallas kernels: 142 us -> 83.8 us
    pallas_call x1, Pallas kernels: 62.4 us -> 4.1 us  [shards(): pl.pallas_call(finals, in_specs=[hbm, vmem], out_specs=(hbm, vmem, vmem),...]
where the time goes in v4:
time: 84.6 us; the launch traced here: 84.5 us
  Pallas kernels  83.8 us (99%)
    pallas_call x1, Pallas kernels, overturning(): pl.pallas_call(functools.partial(kernel, comm), in_specs=[hbm] * 4 + [vme...  79.7 us
    pallas_call x1, Pallas kernels, shards(): pl.pallas_call(finals, in_specs=[hbm, vmem], out_specs=(hbm, vmem, vmem),...  4.1 us

profile of v4, /device:TPU:1, one launch (start us, length us, event | category | flops | bytes accessed | tf_op | source)
XLA Modules:
  0.0 84.5 jit_solution(5653418827257796282)
XLA Ops:
  0.6 79.7 %overturning.1 = (f32[16,2,128,128]{3,2,1,0:T(8,128)}, f32[2,128,128]{2,1,0:T(8,128)}) custom-call(bf16[16,32,32,256]{3,2,1,0:T(8,128)(2,1)} %v_hbm.1, bf16[16,32,32,256]{3,2,1,0:T(8,128)(2,1)} %h_hbm.1, s32[16,32,32,256]{3,2,1,0:T(8,128)} %k_hbm.1, s32[16,32,32,256]{3,2,1,0:T(8,128)} %w_hbm.1, f32[2,128]{1,0:T(2,128)} %bitcast.3), custom_call_target="tpu_custom_call" | custom-call | tf_op jit(solution)/shard_map/overturning/pallas_call | solution.py:479
  80.4 4.1 %finals.1 = (f32[16,120,256]{2,1,0:T(8,128)}, f32[4,120]{1,0:T(4,128)}, f32[4,120]{1,0:T(4,128)}) custom-call(f32[16,2,128,128]{3,2,1,0:T(8,128)} %get-tuple-element.8.pad_hbm, f32[2,128,128]{2,1,0:T(8,128)} %get-tuple-element.9.total), custom_call_target="tpu_custom_call" | custom-call | tf_op jit(solution)/shard_map/finals/pallas_call | solution.py:500

commit v5 on v4

--- a/solution.py
+++ b/solution.py
@@ -17,25 +17,21 @@
 def prepare(raw, turned, chunk):
     lons = pl.ds(chunk * 8, 8)
     cells = pl.ds(pl.multiple_of(chunk * 256, 256), 256)
-    speed, layer, lighter, share = (ref[lons].reshape(256, 256) for ref in raw)
-    v_t, h_t, hi_t, lo_t, q_t, e_t = turned
-    v_t[:, cells] = speed.T
-    h_t[:, cells] = (layer * 64.0).T
-    k = lighter.astype(F32)
-    hi = (k * (1 / 15.0) + (129 - 7 / 15.0)).astype(BF16)
-    hi_t[:, cells] = hi.T
-    lo_t[:, cells] = (k.astype(BF16) - (hi - 129.0) * 15.0).T
-    part = layer.astype(F32) * share.astype(F32)
-    q = part.astype(BF16)
-    q_t[:, cells] = q.T
-    e_t[:, cells] = (part - q.astype(F32)).astype(BF16).T
-
-
-def group_sums(turned, rows, diagonal):
+    for src, dst in zip(raw, turned):
+        dst[:, cells] = src[lons].reshape(256, 256).astype(BF16).T
+
+
+def group_sums(turned, rows):
     total = None
     for start in range(0, 1024, 256):
         cells = slice(start, start + 256)
-        v, h, hi, lo, q, e = (ref[rows, cells] for ref in turned)
+        v, thick, k, w = (ref[rows, cells] for ref in turned)
+        hi = (k.astype(F32) * (1 / 15.0) + (129 - 7 / 15.0)).astype(BF16)
+        lo = k - (hi - 129.0) * 15.0
+        share = thick.astype(F32) * w.astype(F32)
+        q = share.astype(BF16)
+        e = (share - q.astype(F32)).astype(BF16)
+        h = thick * 64.0
         zero = jnp.zeros_like(v)
         a = jnp.concatenate([jnp.where(hi == float(x + 129), v, zero) for x in range(16)], axis=0)
         b, f = [], []
@@ -52,7 +48,35 @@
         )
         total = part if total is None else total + part
     total = total[:256] + total[256:]
-    return jnp.where(diagonal[None], total.reshape(16, 16, 256), 0.0).sum(1)
+    return pick(total)
+
+
+def pick(total):
+    lane = lax.broadcasted_iota(jnp.int32, (8, 128), 1)
+    sub = lax.broadcasted_iota(jnp.int32, (8, 128), 0)
+    blocks = []
+    for start in (0, 128):
+        cols = slice(start, start + 128)
+        upper = (lane & 8) != 0
+        x = [
+            jnp.where(upper, total[16 * i + 8 : 16 * i + 16, cols], total[16 * i : 16 * i + 8, cols])
+            for i in range(16)
+        ]
+        for d in (4, 2, 1):
+            moved = (lane & d) != 0
+            stays = (lane & d) == (sub & d)
+            y = []
+            for i in range(0, len(x), 2 * d):
+                for one, two in zip(x[i : i + d], x[i + d : i + 2 * d]):
+                    keep = jnp.where(moved, two, one)
+                    if d == 4:
+                        move = pltpu.roll(jnp.where(moved, one, two), 4, 0)
+                    else:
+                        move = jnp.where(moved, pltpu.roll(one, 8 - d, 0), pltpu.roll(two, d, 0))
+                    y.append(jnp.where(stays, keep, move))
+            x = y
+        blocks.append(jnp.concatenate(x, axis=0))
+    return jnp.concatenate(blocks, axis=1)
 
 
 def arrange(sums, width, units, slot_of):
@@ -75,7 +99,7 @@
 
 def kernel(comm, v_hbm, h_hbm, k_hbm, w_hbm, width, psi_hbm, total_ref, *scratch):
     (raw_v, raw_h, raw_k, raw_w), scratch = scratch[:4], scratch[4:]
-    even, odd, scratch = scratch[:6], scratch[6:12], scratch[12:]
+    even, odd, scratch = scratch[:4], scratch[4:8], scratch[8:]
     (sums, send, got_1, mid, got_2, own, pad, stat, got_3, read_sem, quarter_sem, write_sem) = scratch[:12]
     (s1, r1, s2, r2, s3, r3, s4, r4, s5, r5) = scratch[12:]
     if comm:
@@ -291,9 +315,6 @@
         greet(None, {"tm": 1 - tm})
     n_greet = 2 * 2 * 4 - 1 + 2 * 2 * 3 + 1
 
-    lane = lax.broadcasted_iota(jnp.int32, (16, 256), 1)
-    row = lax.broadcasted_iota(jnp.int32, (16, 256), 0)
-    diagonal = (lane & 15) == row
     raws = [[ref.at[slot] for ref in (raw_v, raw_h, raw_k, raw_w)] for slot in range(2)]
 
     def quarter(chunk):
@@ -339,15 +360,22 @@
             for copy in read(s + 1, 1 - p):
                 copy.wait()
 
-        def step(j, carry):
-            for c in range(GROUPS // 4):
-                prepare(raws[1 - p], there, j * (GROUPS // 4) + c)
-            for g in range(GROUPS):
-                rows = pl.ds(pl.multiple_of((j * GROUPS + g) * 16, 16), 16)
-                sums[j * GROUPS + g] = group_sums(here, rows, diagonal)
-            return carry
-
-        lax.fori_loop(0, 16 // GROUPS, step, 0)
+        def run(more):
+            def step(j, carry):
+                for c in range(GROUPS // 4 if more else 0):
+                    prepare(raws[1 - p], there, j * (GROUPS // 4) + c)
+                for g in range(GROUPS):
+                    rows = pl.ds(pl.multiple_of((j * GROUPS + g) * 16, 16), 16)
+                    sums[j * GROUPS + g] = group_sums(here, rows)
+                return carry
+
+            lax.fori_loop(0, 16 // GROUPS, step, 0)
+
+        if p == 0:
+            run(True)
+        else:
+            pl.when(s < n_own - 1)(lambda: run(True))
+            pl.when(s == n_own - 1)(lambda: run(False))
         for j in range(2):
             arrange(sums.at[pl.ds(j * 8, 8)], width[j : j + 1, :] * (1 / 64.0), send.at[s], lambda cut: ((cls + cut) % 2) * 2 + j)
 
@@ -431,8 +459,7 @@
 
 def finals(pad_hbm, total, psi_hbm, mean_ref, var_ref, pad, read_sem, sem):
     reads = [
-        pltpu.make_async_copy(pad_hbm.at[pl.ds(4 * i, 4)], pad.at[pl.ds(4 * i, 4)], read_sem.at[i])
-        for i in range(4)
+        pltpu.make_async_copy(pad_hbm.at[s], pad.at[s], read_sem.at[s]) for s in range(16)
     ]
     writes = [
         pltpu.make_async_copy(
@@ -443,15 +470,15 @@
     ]
     for copy in reads:
         copy.start()
+    for s in range(16):
+        reads[s].wait()
+        for copy in writes[2 * s : 2 * s + 2]:
+            copy.start()
     mean = total[0] / 32.0
     var = total[1] / 32.0 - mean * mean
     shift = (128 - lax.axis_index("lon") * 4) % 128
     mean_ref[...] = pltpu.roll(mean, shift, 1).T[:4, : C // 2]
     var_ref[...] = pltpu.roll(var, shift, 1).T[:4, : C // 2]
-    for i in range(4):
-        reads[i].wait()
-        for copy in writes[8 * i : 8 * i + 8]:
-            copy.start()
     for copy in writes:
         copy.wait()
 
@@ -461,7 +488,7 @@
     hbm = pl.BlockSpec(memory_space=pl.ANY)
     vmem = pl.BlockSpec(memory_space=pltpu.VMEM)
     scratch = [pltpu.VMEM((2, 32, 32, 256), d) for d in (BF16, BF16, jnp.int32, jnp.int32)]
-    scratch += [pltpu.VMEM((256, 1024), BF16)] * 12
+    scratch += [pltpu.VMEM((256, 1024), BF16)] * 8
     scratch += [
         pltpu.VMEM((16, 16, 256), F32),
         pltpu.VMEM((8, 4, 128, 128), F32),
@@ -508,7 +535,7 @@
         ),
         scratch_shapes=[
             pltpu.VMEM((16, 2, 128, 128), F32),
-            pltpu.SemaphoreType.DMA((4,)),
+            pltpu.SemaphoreType.DMA((16,)),
             pltpu.SemaphoreType.DMA((16, 2)),
         ],
         compiler_params=pltpu.CompilerParams(vmem_limit_bytes=60 * 2**20),

time: 84.6 us -> 82.2 us (0.972)
  Pallas kernels: 83.8 us -> 81.4 us
    pallas_call x1, Pallas kernels: 79.7 us -> 77.2 us  [overturning(): pl.pallas_call(functools.partial(kernel, comm), in_specs=[hbm] * 4 + [vme...]
where the time goes in v5:
time: 82.2 us; the launch traced here: 82 us
  Pallas kernels  81.4 us (99%)
    pallas_call x1, Pallas kernels, overturning(): pl.pallas_call(functools.partial(kernel, comm), in_specs=[hbm] * 4 + [vme...  77.2 us
    pallas_call x1, Pallas kernels, shards(): pl.pallas_call(finals, in_specs=[hbm, vmem], out_specs=(hbm, vmem, vmem),...  4.16 us

profile of v5, /device:TPU:1, one launch (start us, length us, event | category | flops | bytes accessed | tf_op | source)
XLA Modules:
  0.0 82.0 jit_solution(17073926913652542191)
XLA Ops:
  0.6 77.2 %overturning.1 = (f32[16,2,128,128]{3,2,1,0:T(8,128)}, f32[2,128,128]{2,1,0:T(8,128)}) custom-call(bf16[16,32,32,256]{3,2,1,0:T(8,128)(2,1)} %v_hbm.1, bf16[16,32,32,256]{3,2,1,0:T(8,128)(2,1)} %h_hbm.1, s32[16,32,32,256]{3,2,1,0:T(8,128)} %k_hbm.1, s32[16,32,32,256]{3,2,1,0:T(8,128)} %w_hbm.1, f32[2,128]{1,0:T(2,128)} %bitcast.3), custom_call_target="tpu_custom_call" | custom-call | tf_op jit(solution)/shard_map/overturning/pallas_call | solution.py:506
  77.9 4.2 %finals.1 = (f32[16,120,256]{2,1,0:T(8,128)}, f32[4,120]{1,0:T(4,128)}, f32[4,120]{1,0:T(4,128)}) custom-call(f32[16,2,128,128]{3,2,1,0:T(8,128)} %get-tuple-element.8.pad_hbm, f32[2,128,128]{2,1,0:T(8,128)} %get-tuple-element.9.total), custom_call_target="tpu_custom_call" | custom-call | tf_op jit(solution)/shard_map/finals/pallas_call | solution.py:527

commit v6 on v5

--- a/solution.py
+++ b/solution.py
@@ -89,8 +89,13 @@
             y = list(x)
             for i in range(8):
                 if i & d == 0:
-                    y[i] = jnp.where(high, pltpu.roll(x[i + d], 16 * d, 1), x[i])
-                    y[i + d] = jnp.where(high, x[i + d], pltpu.roll(x[i], 128 - 16 * d, 1))
+                    if d == 4:
+                        move = pltpu.roll(jnp.where(high, x[i], x[i + d]), 64, 1)
+                        y[i] = jnp.where(high, move, x[i])
+                        y[i + d] = jnp.where(high, x[i + d], move)
+                    else:
+                        y[i] = jnp.where(high, pltpu.roll(x[i + d], 16 * d, 1), x[i])
+                        y[i + d] = jnp.where(high, x[i + d], pltpu.roll(x[i], 128 - 16 * d, 1))
             x = y
         for i in range(8):
             units[slot_of(part), 15 * i : 15 * i + 16, :] = (x[i] + offset) * width
@@ -457,7 +462,7 @@
     total_ref[...] = stat[tm] + got_3[...]
 
 
-def finals(pad_hbm, total, psi_hbm, mean_ref, var_ref, pad, read_sem, sem):
+def finals(pad_hbm, total_hbm, psi_hbm, mean_hbm, var_hbm, pad, total, mean_ref, var_ref, read_sem, sem, stat_sem):
     reads = [
         pltpu.make_async_copy(pad_hbm.at[s], pad.at[s], read_sem.at[s]) for s in range(16)
     ]
@@ -468,18 +473,27 @@
         for s in range(16)
         for half in range(2)
     ]
+    sums = pltpu.make_async_copy(total_hbm, total, stat_sem.at[0])
+    stats = [
+        pltpu.make_async_copy(mean_ref, mean_hbm, stat_sem.at[1]),
+        pltpu.make_async_copy(var_ref, var_hbm, stat_sem.at[2]),
+    ]
+    sums.start()
     for copy in reads:
+        copy.start()
+    sums.wait()
+    mean = total[0] / 32.0
+    var = total[1] / 32.0 - mean * mean
+    shift = (128 - lax.axis_index("lon") * 4) % 128
+    mean_ref[...] = pltpu.roll(mean, shift, 1).T[:4, : C // 2]
+    var_ref[...] = pltpu.roll(var, shift, 1).T[:4, : C // 2]
+    for copy in stats:
         copy.start()
     for s in range(16):
         reads[s].wait()
         for copy in writes[2 * s : 2 * s + 2]:
             copy.start()
-    mean = total[0] / 32.0
-    var = total[1] / 32.0 - mean * mean
-    shift = (128 - lax.axis_index("lon") * 4) % 128
-    mean_ref[...] = pltpu.roll(mean, shift, 1).T[:4, : C // 2]
-    var_ref[...] = pltpu.roll(var, shift, 1).T[:4, : C // 2]
-    for copy in writes:
+    for copy in writes + stats:
         copy.wait()
 
 
@@ -526,8 +540,8 @@
     vmem = pl.BlockSpec(memory_space=pltpu.VMEM)
     psi, mean, var = pl.pallas_call(
         finals,
-        in_specs=[hbm, vmem],
-        out_specs=(hbm, vmem, vmem),
+        in_specs=[hbm, hbm],
+        out_specs=(hbm, hbm, hbm),
         out_shape=(
             jax.ShapeDtypeStruct((16, C // 2, 256), F32),
             jax.ShapeDtypeStruct((4, C // 2), F32),
@@ -535,8 +549,12 @@
         ),
         scratch_shapes=[
             pltpu.VMEM((16, 2, 128, 128), F32),
+            pltpu.VMEM((2, 128, 128), F32),
+            pltpu.VMEM((4, C // 2), F32),
+            pltpu.VMEM((4, C // 2), F32),
             pltpu.SemaphoreType.DMA((16,)),
             pltpu.SemaphoreType.DMA((16, 2)),
+            pltpu.SemaphoreType.DMA((3,)),
         ],
         compiler_params=pltpu.CompilerParams(vmem_limit_bytes=60 * 2**20),
         name="finals",

time: 82.2 us -> 80.9 us (0.984)
  Pallas kernels: 81.4 us -> 80.1 us
where the time goes in v6:
time: 80.9 us; the launch traced here: 80.7 us
  Pallas kernels  80.1 us (99%)
    pallas_call x1, Pallas kernels, overturning(): pl.pallas_call(functools.partial(kernel, comm), in_specs=[hbm] * 4 + [vme...  76.6 us
    pallas_call x1, Pallas kernels, shards(): pl.pallas_call(finals, in_specs=[hbm, hbm], out_specs=(hbm, hbm, hbm), ou...  3.46 us

profile of v6, /device:TPU:1, one launch (start us, length us, event | category | flops | bytes accessed | tf_op | source)
XLA Modules:
  0.0 80.7 jit_solution(7134717407014924466)
XLA Ops:
  0.6 76.6 %overturning.1 = (f32[16,2,128,128]{3,2,1,0:T(8,128)}, f32[2,128,128]{2,1,0:T(8,128)}) custom-call(bf16[16,32,32,256]{3,2,1,0:T(8,128)(2,1)} %v_hbm.1, bf16[16,32,32,256]{3,2,1,0:T(8,128)(2,1)} %h_hbm.1, s32[16,32,32,256]{3,2,1,0:T(8,128)} %k_hbm.1, s32[16,32,32,256]{3,2,1,0:T(8,128)} %w_hbm.1, f32[2,128]{1,0:T(2,128)} %bitcast.3), custom_call_target="tpu_custom_call" | custom-call | tf_op jit(solution)/shard_map/overturning/pallas_call | solution.py:520
  77.3 3.5 %finals.1 = (f32[16,120,256]{2,1,0:T(8,128)}, f32[4,120]{1,0:T(4,128)}, f32[4,120]{1,0:T(4,128)}) custom-call(f32[16,2,128,128]{3,2,1,0:T(8,128)} %get-tuple-element.8.pad_hbm, f32[2,128,128]{2,1,0:T(8,128)} %get-tuple-element.9.total_hbm), custom_call_target="tpu_custom_call" | custom-call | tf_op jit(solution)/shard_map/finals/pallas_call | solution.py:541

commit v7 on v6

--- a/solution.py
+++ b/solution.py
@@ -365,6 +365,11 @@
             for copy in read(s + 1, 1 - p):
                 copy.wait()
 
+        def lay_out(j):
+            arrange(
+                sums.at[pl.ds(j * 8, 8)], width[pl.ds(j, 1), :] * (1 / 64.0), send.at[s],
+                lambda cut: ((cls + cut) % 2) * 2 + j)
+
         def run(more):
             def step(j, carry):
                 for c in range(GROUPS // 4 if more else 0):
@@ -372,6 +377,13 @@
                 for g in range(GROUPS):
                     rows = pl.ds(pl.multiple_of((j * GROUPS + g) * 16, 16), 16)
                     sums[j * GROUPS + g] = group_sums(here, rows)
+                if not more:
+                    lay_out(j)
+                    for job in ends:
+                        for rel in (1, 2, 3):
+                            @pl.when(cols[job[1]][rel] % 2 == j)
+                            def _(job=job, rel=rel):
+                                first(job, rel).start()
                 return carry
 
             lax.fori_loop(0, 16 // GROUPS, step, 0)
@@ -381,8 +393,14 @@
         else:
             pl.when(s < n_own - 1)(lambda: run(True))
             pl.when(s == n_own - 1)(lambda: run(False))
-        for j in range(2):
-            arrange(sums.at[pl.ds(j * 8, 8)], width[j : j + 1, :] * (1 / 64.0), send.at[s], lambda cut: ((cls + cut) % 2) * 2 + j)
+        def both():
+            for j in range(2):
+                lay_out(j)
+
+        if p == 0:
+            both()
+        else:
+            pl.when(s < n_own - 1)(both)
 
     def pair(t, carry):
         for p in range(2):
@@ -412,8 +430,6 @@
 
     lax.fori_loop(0, n_own // 2, pair, 0)
     if comm:
-        for job in ends:
-            start_1(job)
         start_2(whole(0, 6))
         start_3(whole(1, 5))
         start_4(whole(0, 4))

time: 80.9 us -> 80.9 us (level)
  no operation moved by 1% of the time
where the time goes in v7:
time: 80.9 us; the launch traced here: 80.7 us
  Pallas kernels  80.1 us (99%)
    pallas_call x1, Pallas kernels, overturning(): pl.pallas_call(functools.partial(kernel, comm), in_specs=[hbm] * 4 + [vme...  76.6 us
    pallas_call x1, Pallas kernels, shards(): pl.pallas_call(finals, in_specs=[hbm, hbm], out_specs=(hbm, hbm, hbm), ou...  3.46 us

profile of v7, /device:TPU:1, one launch (start us, length us, event | category | flops | bytes accessed | tf_op | source)
XLA Modules:
  0.0 80.7 jit_solution(135505741585671729)
XLA Ops:
  0.6 76.6 %overturning.1 = (f32[16,2,128,128]{3,2,1,0:T(8,128)}, f32[2,128,128]{2,1,0:T(8,128)}) custom-call(bf16[16,32,32,256]{3,2,1,0:T(8,128)(2,1)} %v_hbm.1, bf16[16,32,32,256]{3,2,1,0:T(8,128)(2,1)} %h_hbm.1, s32[16,32,32,256]{3,2,1,0:T(8,128)} %k_hbm.1, s32[16,32,32,256]{3,2,1,0:T(8,128)} %w_hbm.1, f32[2,128]{1,0:T(2,128)} %bitcast.3), custom_call_target="tpu_custom_call" | custom-call | tf_op jit(solution)/shard_map/overturning/pallas_call | solution.py:536
  77.2 3.5 %finals.1 = (f32[16,120,256]{2,1,0:T(8,128)}, f32[4,120]{1,0:T(4,128)}, f32[4,120]{1,0:T(4,128)}) custom-call(f32[16,2,128,128]{3,2,1,0:T(8,128)} %get-tuple-element.8.pad_hbm, f32[2,128,128]{2,1,0:T(8,128)} %get-tuple-element.9.total_hbm), custom_call_target="tpu_custom_call" | custom-call | tf_op jit(solution)/shard_map/finals/pallas_call | solution.py:557
